TPU v7x, 32 devices: a whole 2x2x4 slice. The times are simulated.
32 devices in a mesh: tm: 8 (over y, x, core), heads: 4 (over z).
Axes of the slice: x: 2, y: 2, z: 4, core: 2. Of those that a mesh axis runs over, the one named last changes fastest.
Arguments:
- layer_input: bfloat16 [1024, 8192], P('tm', 'heads'), may hold values from -0.119628906 to 0.119628906
- proj_weight: bfloat16 [512, 8192], P('tm', 'heads'), may hold values from -0.0625 to 0.0625
- ssd_input: float32 [1024, 2048], P('tm', 'heads'), may hold values from -0.036 to 0.036
- log_decay: float32 [1024, 32], P('tm', 'heads'), may hold values from -1 to 0, as said below
- out_grad: float32 [1024, 2048], P('tm', 'heads'), may hold values from -15 to 15
Outputs:
- grad_x: float32 [1024, 2048], P('tm', 'heads')
- grad_log: float32 [1024, 32], P('tm', 'heads')
- grad_input: bfloat16 [1024, 8192], P('tm', 'heads')
- grad_weight: float32 [512, 8192], P('tm', 'heads')
Inputs may be any that keep to these rules, and one draw needn't show every extreme that they name: `log_decay`: all entries are negative.
All inputs are finite; a program needn't handle non-finite values.
Results may differ from a plain program's by a relative error of at most 0.023.
Values may be sent and summed in bfloat16 or wider, within the bound.
A program may use at most 64 MiB of HBM per device.

v0:
```python
import jax
import jax.numpy as jnp
from jax import lax
from jax.sharding import PartitionSpec as P

N = 128
SPAN = 128


highest = lax.Precision.HIGHEST


def entering(array, axis, join, neutral):
    place = lax.axis_index(axis)
    gathered = jax.tree.map(
        lambda a, kind: lax.all_gather(a.astype(kind), axis),
        array,
        jax.tree.map(lambda a: jnp.bfloat16 if a.dtype == jnp.float32 else a.dtype, array),
    )
    state = jax.tree.map(lambda a, e: jnp.zeros_like(a) + jnp.asarray(e, a.dtype), array, neutral)

    def one(step, state):
        return join(
            state,
            jax.tree.map(
                lambda a, own: lax.dynamic_index_in_dim(a, step, 0, False).astype(own.dtype),
                gathered,
                array,
            ),
        )

    return lax.fori_loop(0, place, one, state)


def carried_in(array, axis, combine, identity):
    length, index = (lax.axis_size(axis), lax.axis_index(axis))
    everything = jax.tree.map(lambda part: lax.all_gather(part, axis), array)
    start = jax.tree.map(
        lambda part, zero: jnp.broadcast_to(jnp.asarray(zero, part.dtype), part.shape),
        array,
        identity,
    )

    def step(k, before):
        at = length - 1 - k
        reached = at > index
        new = combine(before, jax.tree.map(lambda part: part[at], everything))
        return jax.tree.map(lambda a, b: jnp.where(reached, a, b), new, before)

    return lax.fori_loop(0, length, step, start)


def for_sending(array):
    return jax.tree.map(lambda a: a.astype(jnp.bfloat16) if a.dtype == jnp.float32 else a, array)


def from_partner_2(block, axis, distance):
    count = lax.axis_size(axis)
    route = []
    for low in range(count):
        high = low | 1 << distance
        if high != low and high < count:
            route += [(low, high), (high, low)]
    return lax.ppermute(block, axis, route)


def span_sums(inputs, out_grads, logs, b_rows, c_rows):
    positions = jnp.arange(inputs.shape[0])
    lower_ones = (positions[:, None] >= positions[None, :]).astype(jnp.float32)
    cumlog = jnp.dot(lower_ones, logs, precision=highest)
    decay_sum = cumlog[-1]
    head_state = jnp.einsum(
        "jn,jh,jhp->hnp", b_rows, jnp.exp(decay_sum[None] - cumlog), inputs, precision=highest
    )
    grad_state = jnp.einsum("in,ih,ihp->hnp", c_rows, jnp.exp(cumlog), out_grads, precision=highest)
    return (decay_sum, head_state, grad_state)


def span_grads(inputs, out_grads, logs, b_rows, c_rows, state_in, grad_out):
    positions = jnp.arange(inputs.shape[0])
    causal = positions[:, None] >= positions[None, :]
    lower_ones = causal.astype(jnp.float32)
    strict_ones = (positions[:, None] < positions[None, :]).astype(jnp.float32)
    cumlog = jnp.dot(lower_ones, logs, precision=highest)
    decay_sum = cumlog[-1]
    log_gaps = cumlog.T[:, :, None] - cumlog.T[:, None, :]
    decay_mat = jnp.where(causal[None], jnp.exp(jnp.minimum(log_gaps, 0.0)), 0.0)
    inner_cb = jnp.dot(c_rows, b_rows.T, precision=highest)
    inner_gx = jnp.einsum("ihp,jhp->hij", out_grads, inputs, precision=highest)
    decayed_cb = decay_mat * inner_cb[None]
    decayed_gx = decay_mat * inner_gx
    to_end = jnp.exp(decay_sum[None] - cumlog)
    from_start = jnp.exp(cumlog)
    b_state = jnp.einsum("jn,hnp->jhp", b_rows, grad_out, precision=highest)
    c_state = jnp.einsum("in,hnp->ihp", c_rows, state_in, precision=highest)
    grad_in = (
        jnp.einsum("hij,ihp->jhp", decayed_cb, out_grads, precision=highest)
        + to_end[:, :, None] * b_state
    )
    x_state = jnp.einsum("jhp,hnp->jhn", inputs, grad_out, precision=highest)
    grad_b = jnp.einsum("hij,in->jn", decayed_gx, c_rows, precision=highest) + jnp.einsum(
        "jh,jhn->jn", to_end, x_state, precision=highest
    )
    g_state = jnp.einsum("ihp,hnp->ihn", out_grads, state_in, precision=highest)
    grad_c = jnp.einsum("hij,jn->in", decayed_gx, b_rows, precision=highest) + jnp.einsum(
        "ih,ihn->in", from_start, g_state, precision=highest
    )
    pair_weight = decayed_cb * inner_gx
    prefix_sum = jnp.einsum("hij,jt->hit", pair_weight, strict_ones, precision=highest)
    inside = jnp.einsum("it,hit->th", lower_ones, prefix_sum, precision=highest)
    earlier = from_start * jnp.sum(c_state * out_grads, axis=2)
    later_terms = to_end * jnp.sum(b_state * inputs, axis=2)
    across = jnp.sum(grad_out * state_in, axis=(1, 2)) * jnp.exp(decay_sum)
    grad_log = (
        inside
        + jnp.dot(lower_ones.T, earlier, precision=highest)
        + jnp.dot(strict_ones.T, later_terms, precision=highest)
        + across[None]
    )
    return (grad_in, grad_log, grad_b, grad_c)


def combine(earlier, later):
    return (earlier[0] + later[0], jnp.exp(later[0])[:, None, None] * earlier[1] + later[1])


def on_device(layer_input, proj_weight, ssd_input, log_decay, out_grad):
    weight_cols = lax.all_gather(proj_weight, "tm", axis=0, tiled=True)
    steps_here = layer_input.shape[0]
    group_width = 2 * N
    contract_cols = (((1,), (1,)), ((), ()))
    partial_bc = lax.dot_general(
        layer_input, weight_cols, contract_cols, preferred_element_type=jnp.float32
    )
    head_index = lax.axis_index("heads")
    odd_member = head_index % 2 == 1
    whole_bc = lax.psum(partial_bc, "heads")
    bc_group = lax.dynamic_slice_in_dim(whole_bc, head_index // 2 * group_width, group_width, 1)
    heads_here = log_decay.shape[1]
    head_size = ssd_input.shape[1] // heads_here
    spans = steps_here // SPAN
    inputs = ssd_input.reshape(spans, SPAN, heads_here, head_size)
    out_grads = out_grad.reshape(spans, SPAN, heads_here, head_size)
    logs = log_decay.reshape(spans, SPAN, heads_here)
    b_rows = bc_group[:, :N].reshape(spans, SPAN, N)
    c_rows = bc_group[:, N:].reshape(spans, SPAN, N)
    decay_sums, head_states, grad_states = jax.vmap(span_sums)(
        inputs, out_grads, logs, b_rows, c_rows
    )
    zero_sum = jnp.zeros((heads_here,), jnp.float32)
    zero_state = jnp.zeros((heads_here, N, head_size), jnp.float32)

    def fold_span(carry, item):
        return (combine(carry, item), None)

    local_fwd, _ = lax.scan(fold_span, (zero_sum, zero_state), (decay_sums, head_states))
    local_bwd, _ = lax.scan(
        fold_span, (zero_sum, zero_state), (decay_sums, grad_states), reverse=True
    )
    identity = (zero_sum, zero_state)
    _, slab_state = entering(local_fwd, "tm", combine, identity)
    _, slab_grad = carried_in(local_bwd, "tm", combine, identity)

    def carry_on(carry, item):
        return (jnp.exp(item[0])[:, None, None] * carry + item[1], carry)

    _, states = lax.scan(carry_on, slab_state, (decay_sums, head_states))
    _, grads = lax.scan(carry_on, slab_grad, (decay_sums, grad_states), reverse=True)
    results = lax.map(
        lambda item: span_grads(*item), (inputs, out_grads, logs, b_rows, c_rows, states, grads)
    )
    grad_x = results[0].reshape(steps_here, heads_here * head_size)
    grad_log = results[1].reshape(steps_here, heads_here)
    grad_b = results[2].reshape(steps_here, N)
    grad_c = results[3].reshape(steps_here, N)
    own_half = jnp.where(odd_member, grad_c, grad_b)
    other_half = jnp.where(odd_member, grad_b, grad_c)
    from_partner = from_partner_2(for_sending(other_half), "heads", 0).astype(other_half.dtype)
    grad_half = (own_half + from_partner).astype(jnp.bfloat16)
    grad_bc = lax.all_gather(grad_half, "heads", axis=1, tiled=True)
    grad_input = jnp.dot(grad_bc, weight_cols, preferred_element_type=jnp.float32).astype(
        jnp.bfloat16
    )
    grad_rows = lax.all_to_all(grad_bc, "tm", split_axis=1, concat_axis=0, tiled=True)
    grad_weight = lax.dot_general(
        grad_rows,
        lax.all_gather(layer_input, "tm", axis=0, tiled=True),
        (((0,), (0,)), ((), ())),
        preferred_element_type=jnp.float32,
    )
    return (grad_x, grad_log, grad_input, grad_weight)


def solution(mesh):
    return jax.shard_map(
        on_device,
        mesh=mesh,
        in_specs=(
            P("tm", "heads"),
            P("tm", "heads"),
            P("tm", "heads"),
            P("tm", "heads"),
            P("tm", "heads"),
        ),
        out_specs=(P("tm", "heads"), P("tm", "heads"), P("tm", "heads"), P("tm", "heads")),
        check_vma=False,
    )
```

profile of v0, /device:TPU:1, one launch (start us, length us, event | category | flops | bytes accessed | tf_op | source)
XLA Modules:
  0.0 184.9 jit_solution(11995314810974590621)
XLA Ops:
  7.2 0.7 all-gather.7.cloned.1.call-update
  8.1 0.2 slice_reduce_fusion
  8.4 32.0 %all-gather.7.cloned.1.call-done = bf16[512,2048]{1,0:T(8,128)(2,1)} async-done(((bf16[64,2048]{1,0:T(8,128)(2,1)}), bf16[512,2048]{1,0:T(8,128)(2,1)}) %all-gather.7.cloned.1.call-update) | async-done | bytes 2097168 | tf_op jit(solution)/shard_map/all_gather | solution.py:128
  40.4 3.3 %fusion.64 = f32[128,512]{1,0:T(8,128)} fusion(bf16[128,2048]{1,0:T(8,128)(2,1)} %param.9, bf16[512,2048]{1,0:T(8,128)(2,1)} %all-gather.7.cloned.1.call-done), kind=kOutput, calls=%fused_computation.94 | convolution fusion | flops 268435456 | bytes 2883584 | tf_op jit(solution)/shard_map/dot_general | solution.py:132
  44.0 33.4 %all-reduce.2.cloned.1.call-done = f32[128,512]{1,0:T(8,128)} async-done(((f32[128,512]{1,0:T(8,128)}), f32[128,512]{1,0:T(8,128)}) %all-reduce.2.cloned.1.call-update) | async-done | bytes 262160 | tf_op jit(solution)/shard_map/psum | solution.py:137
  77.4 1.9 %fusion.12 = bf16[1,8,128,64]{2,3,1,0:T(8,128)(2,1)} fusion(f32[128,8,64]{0,2,1:T(8,128)S(1)} %bitcast.119, f32[8]{0:T(128)S(1)} %exponential_multiply_fusion, f32[128,8]{0,1:T(8,128)S(1)} %get-tuple-element.358, f32[128,512]{1,0:T(8,128)} %all-reduce.2.cloned.1.call-done, s32[]{:T(128)S(6)} %select_n.73), kind=kOutput, calls=%fused_computation.25 | convolution fusion | flops 100859904 | bytes 462884 | tf_op jit(solution)/shard_map/vmap(jn,jh,jhp->hnp)/dot_general | solution.py:72
  79.5 1.9 %fusion.9 = f32[1,8,128,64]{2,3,1,0:T(8,128)} fusion(f32[128,8,64]{0,2,1:T(8,128)S(1)} %bitcast.122, f32[128,8]{0,1:T(8,128)S(1)} %get-tuple-element.359, f32[8]{0:T(128)S(1)} %exponential_multiply_fusion, f32[128,512]{1,0:T(8,128)} %all-reduce.2.cloned.1.call-done, s32[]{:T(128)S(6)} %add.160), kind=kOutput, calls=%fused_computation.22 | convolution fusion | flops 100794368 | bytes 593956 | tf_op jit(solution)/shard_map/vmap(in,ih,ihp->hnp)/dot_general | solution.py:75
  81.5 0.5 all-gather.13.cloned.1.call-update
  82.1 0.2 fusion.53
  82.3 10.6 %all-gather = f32[8,1,8]{2,1,0:T(1,128)S(1)} all-gather(f32[1,1,8]{2,1,0:T(1,128)S(1)} %bitcast.133), channel_id=1, replica_groups=mesh['tm'=8,'heads'=4] {'tm'}, dimensions={0}, use_global_device_ids=true | all-gather | bytes 288 | tf_op jit(solution)/shard_map/all_gather | solution.py:37
  92.9 8.7 %all-gather.1 = bf16[8,1,8]{2,1,0:T(2,128)(2,1)S(1)} all-gather(bf16[1,1,8]{2,1,0:T(2,128)(2,1)S(1)} %bitcast.137), channel_id=1, replica_groups=mesh['tm'=8,'heads'=4] {'tm'}, dimensions={0}, use_global_device_ids=true | all-gather | bytes 144 | tf_op jit(solution)/shard_map/all_gather | solution.py:16
  101.6 1.1 multiply_reduce_fusion
  102.7 0.3 fusion.43
  103.0 0.6 fusion.6
  103.5 1.6 all-gather.11.cloned.1.call-done
  105.1 1.3 while.18
  105.2 0.9 constant_dynamic-slice_fusion.4
  106.1 0.2 copy.74
  106.3 0.2 convert_add_fusion.2
  106.5 0.2 copy.32
  106.6 0.6 fusion.5
  107.4 0.4 multiply_reduce_fusion.3
  107.9 0.2 convolution_add_fusion.1
  108.1 27.4 %all-gather.9.cloned.1.call-done = f32[8,8,128,64]{2,3,1,0:T(8,128)} async-done(((f32[1,8,128,64]{2,3,1,0:T(8,128)}), f32[8,8,128,64]{2,3,1,0:T(8,128)}) %all-gather.9.cloned.1.call-update) | async-done | bytes 2097168 | tf_op jit(solution)/shard_map/all_gather | solution.py:37
  135.5 11.0 %while.19 = (s32[]{:T(128)}, f32[8,128,64]{2,1,0:T(8,128)S(1)}, s32[]{:T(128)}, f32[8,8]{1,0:T(8,128)S(1)}, f32[8,8,128,64]{2,3,1,0:T(8,128)}, /*index=5*/s32[]{:T(128)}, s32[]{:T(128)}, s32[]{:T(128)}, s32[]{:T(128)}) while((s32[]{:T(128)}, f32[8,128,64]{2,1,0:T(8,128)S(1)}, s32[]{:T(128)}, f32[8,8]{1,0:T(8,128)S(1)}, ...), condition=%wide.region_2.3_spmd.clone, body=%wide.region_1.2_spmd.clone.sunk | while | flops 262152 | bytes 1835279 | solution.py:50
  135.5 1.0 constant_dynamic-slice_fusion.5
  136.5 0.2 copy.75
  136.7 0.1 fusion.84
  136.9 1.0 constant_dynamic-slice_fusion.5
  137.9 0.2 copy.75
  138.1 0.1 fusion.84
  138.3 1.0 constant_dynamic-slice_fusion.5
  139.2 0.2 copy.75
  139.5 0.1 fusion.84
  139.6 1.0 constant_dynamic-slice_fusion.5
  140.6 0.2 copy.75
  140.9 0.1 fusion.84
  141.0 1.0 constant_dynamic-slice_fusion.5
  142.0 0.2 copy.75
  142.4 1.0 constant_dynamic-slice_fusion.5
  143.4 0.2 copy.75
  143.6 0.1 fusion.84
  143.8 1.0 constant_dynamic-slice_fusion.5
  144.7 0.2 copy.75
  145.0 0.1 fusion.84
  145.1 1.0 constant_dynamic-slice_fusion.5
  146.1 0.2 copy.75
  146.4 0.1 fusion.84
  146.5 0.2 copy.29
  146.7 0.2 multiply_reduce_fusion.1
  146.9 0.6 fusion.4
  147.7 0.3 select_convert_fusion
  148.0 1.3 collective-permute-start
  149.2 0.2 multiply_reduce_fusion.4
  149.4 0.4 multiply_reduce_fusion.2
  149.8 0.8 fusion.7
  150.6 0.8 fusion.13
  151.3 0.8 copy.38
  152.2 9.9 %all_gather.30 = bf16[128,512]{1,0:T(8,128)(2,1)S(1)} all-gather(bf16[128,128]{1,0:T(8,128)(2,1)S(1)} %add_convert_fusion), channel_id=1, replica_groups=mesh['tm'=8,'heads'=4] {'heads'}, dimensions={1}, use_global_device_ids=true | all-gather | bytes 163840 | tf_op jit(solution)/shard_map/all_gather | solution.py:180
  162.1 0.8 copy.36
  162.8 6.3 %all-to-all-start = ((bf16[128,8,64]{0,2,1:T(8,128)(2,1)}), bf16[128,8,64]{0,2,1:T(8,128)(2,1)S(1)}, u32[]{:S(2)}, u32[]{:S(2)}) async-start(bf16[128,8,64]{0,2,1:T(8,128)(2,1)} %bitcast.26), calls=%async_computation | async-start | bytes 262144 | tf_op jit(solution)/shard_map/all_to_all | solution.py:184
  169.1 1.2 convolution_convert_fusion
  170.4 4.1 %all-gather.13.cloned.1.call-done = bf16[1024,2048]{1,0:T(8,128)(2,1)} async-done(((bf16[128,2048]{1,0:T(8,128)(2,1)}), bf16[1024,2048]{1,0:T(8,128)(2,1)}) %all-gather.13.cloned.1.call-update) | async-done | bytes 4194320 | tf_op jit(solution)/shard_map/all_gather | solution.py:187
  174.5 3.8 %fusion.30 = f32[64,2048]{1,0:T(8,128)} fusion(bf16[1024,2048]{1,0:T(8,128)(2,1)} %all-gather.13.cloned.1.call-done, bf16[128,8,64]{0,2,1:T(8,128)(2,1)S(1)} %all-to-all-done), kind=kOutput, calls=%fused_computation.50 | convolution fusion | flops 268435456 | bytes 4849664 | tf_op jit(solution)/shard_map/dot_general | solution.py:185
  (45 shorter events, 1.4 us)
Async XLA Ops:
  7.2 0.8 copy-start
  7.2 36.6 %copy-start.3 = (f32[128,512]{1,0:T(8,128)S(1)}, f32[128,512]{1,0:T(8,128)}, u32[]{:S(2)}) copy-start(f32[128,512]{1,0:T(8,128)} %param.11) | copy-start | bytes 786436
  7.2 33.2 %all-gather.7.cloned.1.call-start = ((), (), s32[]{:S(2)}) async-start(), calls=%async_computation.1 | async-start | bytes 2359296 | tf_op jit(solution)/shard_map/all_gather | solution.py:128
  7.9 69.5 %all-reduce.2.cloned.1.call-start = ((), (), s32[]{:S(2)}) async-start(), calls=%async_computation.2 | async-start | bytes 524288 | tf_op jit(solution)/shard_map/psum | solution.py:137
  8.3 71.0 %copy-start.4 = (f32[128,512]{1,0:T(8,128)S(1)}, f32[128,512]{1,0:T(8,128)}, u32[]{:S(2)}) copy-start(f32[128,512]{1,0:T(8,128)} %param.13) | copy-start | bytes 786436
  43.7 61.4 %all-gather.11.cloned.1.call-start = ((), (), s32[]{:S(2)}) async-start(), calls=%async_computation.4 | async-start | bytes 1179648 | tf_op jit(solution)/shard_map/all_gather | solution.py:16
  77.4 25.3 %copy-start.2 = (f32[128,512]{1,0:T(8,128)S(1)}, f32[128,512]{1,0:T(8,128)}, u32[]{:S(2)}) copy-start(f32[128,512]{1,0:T(8,128)} %all-reduce.2.cloned.1.call-done) | copy-start | bytes 786436
  79.3 56.2 %all-gather.9.cloned.1.call-start = ((), (), s32[]{:S(2)}) async-start(), calls=%async_computation.3 | async-start | bytes 2359296 | tf_op jit(solution)/shard_map/all_gather | solution.py:37
  81.5 93.0 %all-gather.13.cloned.1.call-start = ((), (), s32[]{:S(2)}) async-start(), calls=%async_computation.5 | async-start | bytes 4718592 | tf_op jit(solution)/shard_map/all_gather | solution.py:187
  147.6 21.6 %copy-start.1 = (bf16[512,2048]{1,0:T(8,128)(2,1)S(1)}, bf16[512,2048]{1,0:T(8,128)(2,1)}, u32[]{:S(2)}) copy-start(bf16[512,2048]{1,0:T(8,128)(2,1)} %all-gather.7.cloned.1.call-done) | copy-start | bytes 6291460
  148.0 4.2 %collective-permute-start = (bf16[128,128]{1,0:T(8,128)(2,1)S(1)}, bf16[128,128]{1,0:T(8,128)(2,1)S(1)}, u32[]{:S(2)}, u32[]{:S(2)}) collective-permute-start(bf16[128,128]{1,0:T(8,128)(2,1)S(1)} %get-tuple-element.364), channel_id=1, source_target_pairs={{0,1},{1,0},{2,3},{3,2},{4,5},{5,4},{6,7},{7,6},{8,9},{9,8},{10,11... | collective-permute-start | bytes 98312 | tf_op jit(solution)/shard_map/ppermute | solution.py:64
  162.8 11.7 %all-to-all-start = ((bf16[128,8,64]{0,2,1:T(8,128)(2,1)}), bf16[128,8,64]{0,2,1:T(8,128)(2,1)S(1)}, u32[]{:S(2)}, u32[]{:S(2)}) async-start(bf16[128,8,64]{0,2,1:T(8,128)(2,1)} %bitcast.26), calls=%async_computation | async-start | bytes 262144 | tf_op jit(solution)/shard_map/all_to_all | solution.py:184
Sparse Core Ops, SparseCore 0:
  9.9 30.3 all-gather.6
  43.8 33.5 all-reduce.1
  80.0 25.0 all-gather.10
  107.6 27.9 all-gather.8
  137.4 37.0 all-gather.12
where the time goes:
time: 186 us; the launch traced here: 185 us
  waiting for transfers between devices  99.8 us (54%)
  blocking collectives  29.1 us (16%)
  matrix products  18.4 us (10%)
  between operations  14 us (8%)
  local copies, waits for them, and re-layouts  13.5 us (7%)
  starting transfers between devices  7.77 us (4%)
    psum x1, waiting for transfers between devices, on_device(): whole_bc = lax.psum(partial_bc, 'heads')  33.4 us
    all_gather x1, waiting for transfers between devices, on_device(): weight_cols = lax.all_gather(proj_weight, 'tm', axis=0, tiled=True)  32 us
    all_gather x1, waiting for transfers between devices, carried_in(): everything = jax.tree.map(lambda part: lax.all_gather(part, axis), array)  27.4 us
    all_gather x1, blocking collectives, carried_in(): everything = jax.tree.map(lambda part: lax.all_gather(part, axis), array)  10.6 us
    all_gather x1, blocking collectives, on_device(): grad_bc = lax.all_gather(grad_half, 'heads', axis=1, tiled=True)  9.86 us
    dynamic_slice x16, local copies, waits for them, and re-layouts, step(): new = combine(before, jax.tree.map(lambda part: part[at], everything))  9.4 us
    all_gather x1, blocking collectives, entering(): lax.all_gather(a.astype(kind), axis)  8.69 us
    all_to_all x1, starting transfers between devices, on_device(): lax.all_to_all(grad_bc, 'tm', split_axis=1, concat_axis=0, tiled=True)  6.3 us
  transfers between devices with their start and end apart: 7, of which 5 were waited for; matrix products, arithmetic and copies ran while one was open for 13% of the time, Pallas kernels for 0%

commit v1 on v0

v1 whole, which is shorter than its diff:
```python
import jax
import jax.numpy as jnp
from jax import lax
from jax.experimental import pallas as pl
from jax.experimental.pallas import tpu as pltpu
from jax.sharding import PartitionSpec as P

N = 128
MESH = pl.DeviceIdType.MESH
HIGH = lax.Precision.HIGHEST
F32 = jnp.float32
BF16 = jnp.bfloat16


def nn(a, b, precision=None):
    return lax.dot_general(
        a, b, (((1,), (0,)), ((), ())), precision=precision, preferred_element_type=F32
    )


def nt(a, b, precision=None):
    return lax.dot_general(
        a, b, (((1,), (1,)), ((), ())), precision=precision, preferred_element_type=F32
    )


class Gather:
    def __init__(self, buf, send, recv, tm, me, heads_at):
        self.buf, self.send, self.recv = buf, send, recv
        self.tm, self.me, self.z = tm, me, heads_at
        self.chips = tm // 2
        self.chip, self.core = me // 2, lax.rem(me, 2)
        self.half_rows = buf.shape[1] // 2
        self.pending = []
        chip = self.chip
        if self.chips == 4:
            self.xn = chip + 1 - 2 * lax.rem(chip, 2)
            self.yn = lax.rem(chip + 2, 4)
            self.dg = 3 - chip

    def piece(self, slot, half):
        return self.buf.at[slot, pl.ds(half * self.half_rows, self.half_rows)]

    def copy(self, slot, half, chip, core, number):
        part = self.piece(slot, half)
        return pltpu.make_async_remote_copy(
            src_ref=part,
            dst_ref=part,
            send_sem=self.send.at[number],
            recv_sem=self.recv.at[slot, half],
            device_id=(chip * 2 + core, self.z),
            device_id_type=MESH,
        )

    def push(self, slot, half, chip, core):
        made = self.copy(slot, half, chip, core, len(self.pending))
        made.start()
        self.pending.append(made)

    def arrive(self, slot, half):
        self.copy(slot, half, self.chip, 1 - self.core, 0).wait_recv()

    def start(self):
        me, core = self.me, self.core
        if self.chips == 4:
            self.push(me, 0, self.xn, core)
            self.push(me, 1, self.yn, core)
            self.push(me, 1, self.xn, core)
            self.push(me, 0, self.yn, core)
        else:
            for d in range(1, self.chips):
                for half in range(2):
                    self.push(me, half, lax.rem(self.chip + d, self.chips), core)
        for half in range(2):
            self.push(me, half, self.chip, 1 - core)

    def near(self):
        core = self.core
        if self.chips == 4:
            xs, ys = self.xn * 2 + core, self.yn * 2 + core
            self.arrive(xs, 0)
            self.push(xs, 0, self.yn, core)
            self.arrive(ys, 1)
            self.push(ys, 1, self.xn, core)
            self.push(xs, 0, self.chip, 1 - core)
            self.push(ys, 1, self.chip, 1 - core)
            self.arrive(xs, 1)
            self.push(xs, 1, self.chip, 1 - core)
            self.arrive(ys, 0)
            self.push(ys, 0, self.chip, 1 - core)

    def far(self):
        core = self.core
        if self.chips == 4:
            slots = [self.dg * 2 + core]
        else:
            slots = [lax.rem(self.chip + d, self.chips) * 2 + core for d in range(1, self.chips)]
        for slot in slots:
            for half in range(2):
                self.arrive(slot, half)
                self.push(slot, half, self.chip, 1 - core)

    def other(self, chip):
        for half in range(2):
            self.arrive(chip * 2 + 1 - self.core, half)

    def finish(self):
        for made in self.pending:
            made.wait_send()


def exchange(src, dst, send, recv, count, me, place):
    copies = []
    for d in range(1, count):
        to = lax.rem(me + d, count)
        copies.append(
            pltpu.make_async_remote_copy(
                src_ref=src(d, to),
                dst_ref=dst.at[me],
                send_sem=send.at[d],
                recv_sem=recv.at[me],
                device_id=place(to),
                device_id_type=MESH,
            )
        )
    for made in copies:
        made.start()
    return copies


def landed(dst, send, recv, slot, to):
    return pltpu.make_async_remote_copy(
        src_ref=dst.at[slot],
        dst_ref=dst.at[slot],
        send_sem=send.at[0],
        recv_sem=recv.at[slot],
        device_id=to,
        device_id_type=MESH,
    )


def kernel(
    tm, heads, members,
    li_ref, w_ref, x_ref, log_ref, dy_ref,
    gx_ref, gl_ref, gi_ref, gw_ref,
    wbuf, libuf, dec, pbuf, bcr, st, strecv, hin, gout, decay, dgx, gbuf, grecv, gall, grow,
    w_send, w_recv, li_send, li_recv, d_send, d_recv, p_send, p_recv, s_send, s_recv,
    g_send, g_recv, a_send, a_recv,
):
    me = lax.axis_index("tm")
    z = lax.axis_index("heads")
    chips = tm // 2
    span = li_ref.shape[0]
    heads_here = log_ref.shape[1]
    width = x_ref.shape[1]
    size = width // heads_here
    rows_w = w_ref.shape[0]
    along = lambda to: (to, z)
    across_z = lambda to: (me, to)
    peer = (lax.rem(me + 1, tm), z)

    barrier = pltpu.get_barrier_semaphore()
    for d in range(1, tm):
        pl.semaphore_signal(
            barrier, inc=1, device_id=along(lax.rem(me + d, tm)), device_id_type=MESH
        )
    for d in range(1, heads):
        pl.semaphore_signal(
            barrier, inc=1, device_id=across_z(lax.rem(z + d, heads)), device_id_type=MESH
        )
    wbuf[me] = w_ref[...]
    libuf[me] = li_ref[...]
    pl.semaphore_wait(barrier, tm - 1 + heads - 1)

    weights = Gather(wbuf, w_send, w_recv, tm, me, z)
    layer = Gather(libuf, li_send, li_recv, tm, me, z)
    weights.start()
    started = []

    row = lax.broadcasted_iota(jnp.int32, (span, span), 0)
    col = lax.broadcasted_iota(jnp.int32, (span, span), 1)
    lower = (row >= col).astype(F32)
    upper = (row <= col).astype(F32)
    strict = (row > col).astype(F32)
    head_of = lax.broadcasted_iota(jnp.int32, (heads_here, width), 0) * size
    place = lax.broadcasted_iota(jnp.int32, (heads_here, width), 1)
    spread = ((place >= head_of) & (place < head_of + size)).astype(F32)
    logs = log_ref[...]
    sums = nn(lower, logs, HIGH)
    sums_t = sums.T
    wide = nn(lower, nn(logs, spread, HIGH), HIGH)
    total = wide[span - 1 : span, :]
    dec[me] = jnp.broadcast_to(total, (8, width))
    started += exchange(lambda d, to: dec.at[me], dec, d_send, d_recv, tm, me, along)
    from_start = jnp.exp(wide)
    to_end = jnp.exp(total - wide)
    x = x_ref[...]
    dy = dy_ref[...]
    x_end = (to_end * x).astype(BF16)
    dy_start = (from_start * dy).astype(BF16)
    x_half = x.astype(BF16)
    dy_half = dy.astype(BF16)

    dgx_sum = jnp.zeros((span, span), F32)
    for h in range(heads_here):
        cut = slice(h * size, (h + 1) * size)
        gaps = sums_t[h : h + 1, :] - sums[:, h : h + 1]
        step = jnp.where(row <= col, jnp.exp(jnp.minimum(gaps, 0.0)), 0.0)
        pairs = step * nt(x_half[:, cut], dy_half[:, cut])
        decay[h] = step
        dgx[h] = pairs
        dgx_sum = dgx_sum + pairs

    def project(chip):
        block = wbuf[pl.ds(2 * chip, 2)].reshape(2 * rows_w, wbuf.shape[2])
        pbuf[chip] = nt(li_ref[...], block).astype(BF16)

    weights.near()
    weights.other(weights.chip)
    project(weights.chip)
    if chips == 4:
        weights.other(weights.xn)
        project(weights.xn)
        weights.other(weights.yn)
        project(weights.yn)
        weights.far()
        weights.other(weights.dg)
        project(weights.dg)
    else:
        weights.far()
        for d in range(1, chips):
            chip = lax.rem(weights.chip + d, chips)
            weights.other(chip)
            project(chip)
    group = z // members
    bcr[z] = pbuf[pl.ds(2 * group, 2)]
    started += exchange(
        lambda d, to: pbuf.at[pl.ds(2 * (to // members), 2)], bcr, p_send, p_recv, heads, z, across_z
    )
    layer.start()
    for d in range(1, heads):
        landed(bcr, p_send, p_recv, lax.rem(z + d, heads), peer).wait_recv()
    bc = bcr[0].astype(F32)
    for k in range(1, heads):
        bc = bc + bcr[k].astype(F32)
    b_t = bc[0].T.astype(BF16)
    c_t = bc[1].T.astype(BF16)
    b = bc[0].astype(BF16)
    c = bc[1].astype(BF16)

    st[0] = nn(b_t, x_end).astype(BF16)
    st[1] = nn(c_t, dy_start).astype(BF16)
    started += exchange(
        lambda d, to: st.at[(me + d) // tm], strecv, s_send, s_recv, tm, me, along
    )

    cb = nt(b, c)
    after = []
    before = []
    for h in range(heads_here):
        cut = slice(h * size, (h + 1) * size)
        weight = decay[h] * cb
        gx_ref[:, cut] = nn(weight.astype(BF16), dy_half[:, cut])
        product = dgx[h] * cb
        after.append(jnp.sum(product, axis=1, keepdims=True))
        before.append(jnp.sum(product, axis=0, keepdims=True))
    before = jnp.concatenate(before, axis=0)
    after = jnp.concatenate(after, axis=1)
    grad_b = nn(c_t, dgx_sum.T.astype(BF16))
    grad_c = nn(b_t, dgx_sum.astype(BF16))
    inside = nn(strict, after, HIGH) - nt(strict, before, HIGH)

    hin[...] = jnp.zeros_like(hin)
    gout[...] = jnp.zeros_like(gout)

    def forward(q, _):
        landed(dec, d_send, d_recv, q, peer).wait_recv()
        landed(strecv, s_send, s_recv, q, peer).wait_recv()
        hin[...] = hin[...] * jnp.exp(dec[q][0:1, :]) + strecv[q].astype(F32)
        return 0

    def backward(k, _):
        q = tm - 1 - k
        landed(dec, d_send, d_recv, q, peer).wait_recv()
        landed(strecv, s_send, s_recv, q, peer).wait_recv()
        gout[...] = gout[...] * jnp.exp(dec[q][0:1, :]) + strecv[q].astype(F32)
        return 0

    lax.fori_loop(0, me, forward, 0)
    lax.fori_loop(0, tm - 1 - me, backward, 0)
    state = hin[...]
    grad = gout[...]
    state_half = state.astype(BF16)
    grad_half = grad.astype(BF16)
    gbuf[0] = (grad_b + nt(grad_half, x_end)).astype(BF16)
    gbuf[1] = (grad_c + nt(state_half, dy_start)).astype(BF16)
    grecv[z] = gbuf[...]
    started += exchange(lambda d, to: gbuf, grecv, g_send, g_recv, heads, z, across_z)

    from_end = to_end * nn(b, grad_half)
    gx_ref[...] += from_end
    earlier = nt(from_start * nn(c, state_half) * dy, spread, HIGH)
    later = nt(from_end * x, spread, HIGH)
    through = jnp.sum(grad * state, axis=0, keepdims=True) * jnp.exp(total)
    through = nt(jnp.broadcast_to(through, (8, width)), spread, HIGH)
    gl_ref[...] = (
        inside + nn(upper, earlier, HIGH) + nn(strict, later, HIGH) + through[0:1, :]
    )
    layer.near()

    for d in range(1, heads):
        landed(grecv, g_send, g_recv, lax.rem(z + d, heads), peer).wait_recv()
    turned = []
    for g in range(heads // members):
        for part in range(2):
            acc = grecv[g * members, part].astype(F32)
            for k in range(1, members):
                acc = acc + grecv[g * members + k, part].astype(F32)
            piece = acc.astype(BF16)
            first = (2 * g + part) * N // rows_w
            for k in range(N // rows_w):
                gall[first + k] = piece[k * rows_w : (k + 1) * rows_w]
            turned.append(piece.astype(F32).T.astype(BF16))
    started += exchange(lambda d, to: gall.at[to], grow, a_send, a_recv, tm, me, along)
    grow[me] = gall[me]
    layer.far()
    grad_bc = jnp.concatenate(turned, axis=1)
    gi_ref[...] = nn(grad_bc, wbuf[...].reshape(tm * rows_w, wbuf.shape[2])).astype(BF16)

    layer.other(layer.chip)
    for d in range(1, chips):
        layer.other(lax.rem(layer.chip + d, chips))
    for d in range(1, tm):
        landed(grow, a_send, a_recv, lax.rem(me + d, tm), peer).wait_recv()
    rows = jnp.concatenate([grow[k] for k in range(tm)], axis=1)
    gw_ref[...] = nn(rows, libuf[...].reshape(tm * span, libuf.shape[2]))

    for made in started:
        made.wait_send()
    weights.finish()
    layer.finish()


def solution(mesh):
    tm = mesh.shape["tm"]
    heads = mesh.shape["heads"]
    chips = tm // 2

    def on_device(layer_input, proj_weight, ssd_input, log_decay, out_grad):
        span, depth = layer_input.shape
        rows_w = proj_weight.shape[0]
        heads_here = log_decay.shape[1]
        width = ssd_input.shape[1]
        groups = rows_w * tm // (2 * N)
        members = heads // groups
        copies = 14 if chips == 4 else 4 * (chips - 1) + 2
        dma = lambda *shape: pltpu.SemaphoreType.DMA(shape)
        vmem = pl.BlockSpec(memory_space=pltpu.VMEM)

        def body(*refs):
            kernel(tm, heads, members, *refs)

        return pl.pallas_call(
            body,
            out_shape=(
                jax.ShapeDtypeStruct((span, width), F32),
                jax.ShapeDtypeStruct((span, heads_here), F32),
                jax.ShapeDtypeStruct((span, depth), BF16),
                jax.ShapeDtypeStruct((rows_w, depth), F32),
            ),
            in_specs=[vmem] * 5,
            out_specs=(vmem,) * 4,
            scratch_shapes=[
                pltpu.VMEM((tm, rows_w, depth), BF16),
                pltpu.VMEM((tm, span, depth), BF16),
                pltpu.VMEM((tm, 8, width), F32),
                pltpu.VMEM((chips, span, N), BF16),
                pltpu.VMEM((heads, 2, span, N), BF16),
                pltpu.VMEM((2, N, width), BF16),
                pltpu.VMEM((tm, N, width), BF16),
                pltpu.VMEM((N, width), F32),
                pltpu.VMEM((N, width), F32),
                pltpu.VMEM((heads_here, span, span), F32),
                pltpu.VMEM((heads_here, span, span), F32),
                pltpu.VMEM((2, N, span), BF16),
                pltpu.VMEM((heads, 2, N, span), BF16),
                pltpu.VMEM((tm, rows_w, span), BF16),
                pltpu.VMEM((tm, rows_w, span), BF16),
                dma(copies), dma(tm, 2),
                dma(copies), dma(tm, 2),
                dma(tm), dma(tm),
                dma(heads), dma(heads),
                dma(tm), dma(tm),
                dma(heads), dma(heads),
                dma(tm), dma(tm),
            ],
            compiler_params=pltpu.CompilerParams(
                collective_id=0, has_side_effects=True, vmem_limit_bytes=48 * 1024 * 1024
            ),
        )(layer_input, proj_weight, ssd_input, log_decay, out_grad)

    return jax.shard_map(
        on_device,
        mesh=mesh,
        in_specs=(P("tm", "heads"),) * 5,
        out_specs=(P("tm", "heads"),) * 4,
        check_vma=False,
    )
```

time: 186 us -> 62.6 us (0.34)
  waiting for transfers between devices: 99.8 us -> 0 us
  Pallas kernels: 0 us -> 53.4 us
  blocking collectives: 29.1 us -> 0 us
  matrix products: 18.4 us -> 0 us
  between operations: 14 us -> 0.65 us
  starting transfers between devices: 7.77 us -> 0 us
  local copies, waits for them, and re-layouts: 13.5 us -> 7.62 us
    all_gather x4 -> x0, waiting for transfers between devices: 65.1 us -> none  [the longest x1 32 us: on_device(): weight_cols = lax.all_gather(proj_weight, 'tm', axis=0, tiled=True)]
    pallas_call x0 -> x1, Pallas kernels: none -> 53.4 us  [on_device(): pl.pallas_call(body, out_shape=(jax.ShapeDtypeStruct((span, width), F32),...]
    psum x1 -> x0, waiting for transfers between devices: 33.4 us -> none  [on_device(): whole_bc = lax.psum(partial_bc, 'heads')]
    all_gather x3 -> x0, blocking collectives: 29.1 us -> none  [the longest x1 10.6 us: carried_in(): everything = jax.tree.map(lambda part: lax.all_gather(part, axis), array)]
    dot_general x16 -> x0, matrix products: 17.6 us -> none  [the longest x1 3.85 us: on_device(): lax.dot_general(grad_rows, lax.all_gather(layer_input, 'tm', axis=0, tile...]
    dynamic_slice x18 -> x0, local copies, waits for them, and re-layouts: 10.5 us -> none  [the longest x16 9.4 us: step(): new = combine(before, jax.tree.map(lambda part: part[at], everything))]
    all_to_all x1 -> x0, starting transfers between devices: 6.3 us -> none  [on_device(): lax.all_to_all(grad_bc, 'tm', split_axis=1, concat_axis=0, tiled=True)]
    unnamed x14 -> x12, local copies, waits for them, and re-layouts: 1.11 us -> 6.96 us
  transfers between devices with their start and end apart: 7 -> 0, of which waited for: 5 -> 0; matrix products, arithmetic and copies ran while one was open for 13% -> 0% of each run, Pallas kernels for 0% -> 0%
where the time goes in v1:
time: 62.6 us; the launch traced here: 61.7 us
  Pallas kernels  53.4 us (85%)
  local copies, waits for them, and re-layouts  7.62 us (12%)
  between operations  0.65 us (1%)
    pallas_call x1, Pallas kernels, on_device(): pl.pallas_call(body, out_shape=(jax.ShapeDtypeStruct((span, width), F32),...  53.4 us
    unnamed x12, local copies, waits for them, and re-layouts  6.96 us

profile of v1, /device:TPU:1, one launch (start us, length us, event | category | flops | bytes accessed | tf_op | source)
XLA Modules:
  0.0 61.7 jit_solution(10447843627834413161)
XLA Ops:
  0.6 0.8 %copy.9.refs_3_ = f32[128,8]{1,0:T(8,128)S(1)} copy(f32[128,8]{0,1:T(8,128)} %param.8) | data formatting | bytes 8192 | tf_op args[3]
  1.4 0.0 copy-start
  1.4 1.0 %copy-done = bf16[128,2048]{1,0:T(8,128)(2,1)S(1)} copy-done((bf16[128,2048]{1,0:T(8,128)(2,1)S(1)}, bf16[128,2048]{1,0:T(8,128)(2,1)}, u32[]{:S(2)}) %copy-start) | copy-done | bytes 524312
  2.5 0.0 copy-start.1
  2.5 0.9 %copy-done.1 = bf16[64,2048]{1,0:T(8,128)(2,1)S(1)} copy-done((bf16[64,2048]{1,0:T(8,128)(2,1)S(1)}, bf16[64,2048]{1,0:T(8,128)(2,1)}, u32[]{:S(2)}) %copy-start.1) | copy-done | bytes 262168
  3.4 0.0 copy-start.2
  3.4 0.9 %copy-done.2 = f32[128,512]{1,0:T(8,128)S(1)} copy-done((f32[128,512]{1,0:T(8,128)S(1)}, f32[128,512]{1,0:T(8,128)}, u32[]{:S(2)}) %copy-start.2) | copy-done | bytes 262168
  4.4 0.0 copy-start.3
  4.4 0.9 %copy-done.3 = f32[128,512]{1,0:T(8,128)S(1)} copy-done((f32[128,512]{1,0:T(8,128)S(1)}, f32[128,512]{1,0:T(8,128)}, u32[]{:S(2)}) %copy-start.3) | copy-done | bytes 262168
  5.3 53.4 %shard_map.84 = (f32[128,512]{1,0:T(8,128)S(1)}, f32[128,8]{1,0:T(8,128)S(1)}, bf16[128,2048]{1,0:T(8,128)(2,1)S(1)}, f32[64,2048]{1,0:T(8,128)S(1)}) custom-call(bf16[128,2048]{1,0:T(8,128)(2,1)S(1)} %copy-done, bf16[64,2048]{1,0:T(8,128)(2,1)S(1)} %copy-done.1, f32[128,512]{1,0:T(8,128)S(1)} %copy-done.2, f32[128,8]{1,0:T(8,128)S(1)} %copy.9.refs_3_, ...), custom_call_target="tpu_custom_call" | custom-call | tf_op jit(solution)/shard_map/pallas_call | solution.py:363
  58.7 0.7 %copy.10 = f32[128,8]{0,1:T(8,128)} copy(f32[128,8]{1,0:T(8,128)S(1)} %get-tuple-element.5) | data formatting | bytes 8192 | tf_op jit(solution)/shard_map/pallas_call | solution.py:363
  59.4 0.7 %copy.14 = f32[128,512]{1,0:T(8,128)} copy(f32[128,512]{1,0:T(8,128)S(1)} %get-tuple-element.12) | data formatting | bytes 524288
  60.1 0.8 %copy.15 = bf16[128,2048]{1,0:T(8,128)(2,1)} copy(bf16[128,2048]{1,0:T(8,128)(2,1)S(1)} %get-tuple-element.14) | data formatting | bytes 1048576
  60.9 0.8 %copy.16 = f32[64,2048]{1,0:T(8,128)} copy(f32[64,2048]{1,0:T(8,128)S(1)} %get-tuple-element.15) | data formatting | bytes 1048576
Async XLA Ops:
  1.4 1.0 %copy-start = (bf16[128,2048]{1,0:T(8,128)(2,1)S(1)}, bf16[128,2048]{1,0:T(8,128)(2,1)}, u32[]{:S(2)}) copy-start(bf16[128,2048]{1,0:T(8,128)(2,1)} %refs_0_.1) | copy-start | bytes 1572868
  2.5 0.9 %copy-start.1 = (bf16[64,2048]{1,0:T(8,128)(2,1)S(1)}, bf16[64,2048]{1,0:T(8,128)(2,1)}, u32[]{:S(2)}) copy-start(bf16[64,2048]{1,0:T(8,128)(2,1)} %refs_1_.1) | copy-start | bytes 786436
  3.4 0.9 %copy-start.2 = (f32[128,512]{1,0:T(8,128)S(1)}, f32[128,512]{1,0:T(8,128)}, u32[]{:S(2)}) copy-start(f32[128,512]{1,0:T(8,128)} %refs_2_.1) | copy-start | bytes 786436
  4.4 0.9 %copy-start.3 = (f32[128,512]{1,0:T(8,128)S(1)}, f32[128,512]{1,0:T(8,128)}, u32[]{:S(2)}) copy-start(f32[128,512]{1,0:T(8,128)} %refs_4_.1) | copy-start | bytes 786436

commit v2 on v1

--- a/solution.py
+++ b/solution.py
@@ -61,20 +61,30 @@
         self.copy(slot, half, self.chip, 1 - self.core, 0).wait_recv()
 
     def start(self):
+        self.first()
+        self.second()
+
+    def first(self):
         me, core = self.me, self.core
         if self.chips == 4:
             self.push(me, 0, self.xn, core)
             self.push(me, 1, self.yn, core)
+        else:
+            for d in range(1, self.chips):
+                self.push(me, 0, lax.rem(self.chip + d, self.chips), core)
+        for half in range(2):
+            self.push(me, half, self.chip, 1 - core)
+
+    def second(self):
+        me, core = self.me, self.core
+        if self.chips == 4:
             self.push(me, 1, self.xn, core)
             self.push(me, 0, self.yn, core)
         else:
             for d in range(1, self.chips):
-                for half in range(2):
-                    self.push(me, half, lax.rem(self.chip + d, self.chips), core)
-        for half in range(2):
-            self.push(me, half, self.chip, 1 - core)
-
-    def near(self):
+                self.push(me, 1, lax.rem(self.chip + d, self.chips), core)
+
+    def relay(self):
         core = self.core
         if self.chips == 4:
             xs, ys = self.xn * 2 + core, self.yn * 2 + core
@@ -84,6 +94,11 @@
             self.push(ys, 1, self.xn, core)
             self.push(xs, 0, self.chip, 1 - core)
             self.push(ys, 1, self.chip, 1 - core)
+
+    def near(self):
+        core = self.core
+        if self.chips == 4:
+            xs, ys = self.xn * 2 + core, self.yn * 2 + core
             self.arrive(xs, 1)
             self.push(xs, 1, self.chip, 1 - core)
             self.arrive(ys, 0)
@@ -141,24 +156,34 @@
 
 def kernel(
     tm, heads, members,
-    li_ref, w_ref, x_ref, log_ref, dy_ref,
+    li_hbm, w_hbm, x_hbm, log_hbm, dy_hbm,
     gx_ref, gl_ref, gi_ref, gw_ref,
+    x_ref, dy_ref, log_ref,
     wbuf, libuf, dec, pbuf, bcr, st, strecv, hin, gout, decay, dgx, gbuf, grecv, gall, grow,
     w_send, w_recv, li_send, li_recv, d_send, d_recv, p_send, p_recv, s_send, s_recv,
-    g_send, g_recv, a_send, a_recv,
+    g_send, g_recv, a_send, a_recv, in_sem,
 ):
     me = lax.axis_index("tm")
     z = lax.axis_index("heads")
     chips = tm // 2
-    span = li_ref.shape[0]
-    heads_here = log_ref.shape[1]
+    span = li_hbm.shape[0]
+    heads_here = log_ref.shape[0]
     width = x_ref.shape[1]
     size = width // heads_here
-    rows_w = w_ref.shape[0]
+    rows_w = w_hbm.shape[0]
     along = lambda to: (to, z)
     across_z = lambda to: (me, to)
     peer = (lax.rem(me + 1, tm), z)
 
+    loads = [
+        pltpu.make_async_copy(src, dst, in_sem.at[k])
+        for k, (src, dst) in enumerate((
+            (log_hbm, log_ref), (w_hbm, wbuf.at[me]), (x_hbm, x_ref), (dy_hbm, dy_ref),
+            (li_hbm, libuf.at[me]),
+        ))
+    ]
+    for made in loads:
+        made.start()
     barrier = pltpu.get_barrier_semaphore()
     for d in range(1, tm):
         pl.semaphore_signal(
@@ -168,13 +193,9 @@
         pl.semaphore_signal(
             barrier, inc=1, device_id=across_z(lax.rem(z + d, heads)), device_id_type=MESH
         )
-    wbuf[me] = w_ref[...]
-    libuf[me] = li_ref[...]
-    pl.semaphore_wait(barrier, tm - 1 + heads - 1)
 
     weights = Gather(wbuf, w_send, w_recv, tm, me, z)
     layer = Gather(libuf, li_send, li_recv, tm, me, z)
-    weights.start()
     started = []
 
     row = lax.broadcasted_iota(jnp.int32, (span, span), 0)
@@ -185,13 +206,18 @@
     head_of = lax.broadcasted_iota(jnp.int32, (heads_here, width), 0) * size
     place = lax.broadcasted_iota(jnp.int32, (heads_here, width), 1)
     spread = ((place >= head_of) & (place < head_of + size)).astype(F32)
-    logs = log_ref[...]
-    sums = nn(lower, logs, HIGH)
-    sums_t = sums.T
-    wide = nn(lower, nn(logs, spread, HIGH), HIGH)
+    loads[0].wait()
+    sums_t = nn(log_ref[...], upper, HIGH)
+    sums = sums_t.T
+    wide = nn(sums, spread, HIGH)
     total = wide[span - 1 : span, :]
     dec[me] = jnp.broadcast_to(total, (8, width))
+    loads[1].wait()
+    pl.semaphore_wait(barrier, tm - 1 + heads - 1)
+    weights.start()
     started += exchange(lambda d, to: dec.at[me], dec, d_send, d_recv, tm, me, along)
+    loads[2].wait()
+    loads[3].wait()
     from_start = jnp.exp(wide)
     to_end = jnp.exp(total - wide)
     x = x_ref[...]
@@ -200,6 +226,8 @@
     dy_start = (from_start * dy).astype(BF16)
     x_half = x.astype(BF16)
     dy_half = dy.astype(BF16)
+
+    weights.relay()
 
     dgx_sum = jnp.zeros((span, span), F32)
     for h in range(heads_here):
@@ -211,9 +239,28 @@
         dgx[h] = pairs
         dgx_sum = dgx_sum + pairs
 
+    loads[4].wait()
+    sent = []
+
     def project(chip):
+        number = len(sent)
         block = wbuf[pl.ds(2 * chip, 2)].reshape(2 * rows_w, wbuf.shape[2])
-        pbuf[chip] = nt(li_ref[...], block).astype(BF16)
+        pbuf[chip] = nt(libuf[me], block).astype(BF16)
+        part = lax.rem(chip, 2)
+        made = []
+        for m in range(members):
+            to = chip // 2 * members + m
+            made.append((to, pltpu.make_async_remote_copy(
+                src_ref=pbuf.at[chip],
+                dst_ref=bcr.at[z, part],
+                send_sem=p_send.at[number, m],
+                recv_sem=p_recv.at[z, part],
+                device_id=across_z(to),
+                device_id_type=MESH,
+            )))
+        sent.append(made)
+        for to, copy in made:
+            pl.when(to != z)(copy.start)
 
     weights.near()
     weights.other(weights.chip)
@@ -224,22 +271,29 @@
         weights.other(weights.yn)
         project(weights.yn)
         weights.far()
+        layer.first()
         weights.other(weights.dg)
         project(weights.dg)
     else:
         weights.far()
+        layer.first()
         for d in range(1, chips):
             chip = lax.rem(weights.chip + d, chips)
             weights.other(chip)
             project(chip)
     group = z // members
     bcr[z] = pbuf[pl.ds(2 * group, 2)]
-    started += exchange(
-        lambda d, to: pbuf.at[pl.ds(2 * (to // members), 2)], bcr, p_send, p_recv, heads, z, across_z
-    )
-    layer.start()
     for d in range(1, heads):
-        landed(bcr, p_send, p_recv, lax.rem(z + d, heads), peer).wait_recv()
+        other = lax.rem(z + d, heads)
+        for part in range(2):
+            pltpu.make_async_remote_copy(
+                src_ref=bcr.at[other, part],
+                dst_ref=bcr.at[other, part],
+                send_sem=p_send.at[0, 0],
+                recv_sem=p_recv.at[other, part],
+                device_id=peer,
+                device_id_type=MESH,
+            ).wait_recv()
     bc = bcr[0].astype(F32)
     for k in range(1, heads):
         bc = bc + bcr[k].astype(F32)
@@ -250,9 +304,24 @@
 
     st[0] = nn(b_t, x_end).astype(BF16)
     st[1] = nn(c_t, dy_start).astype(BF16)
-    started += exchange(
-        lambda d, to: st.at[(me + d) // tm], strecv, s_send, s_recv, tm, me, along
-    )
+    chip, core = me // 2, lax.rem(me, 2)
+
+    def state_copy(src, slot, to, number):
+        made = pltpu.make_async_remote_copy(
+            src_ref=src,
+            dst_ref=strecv.at[slot],
+            send_sem=s_send.at[number],
+            recv_sem=s_recv.at[slot],
+            device_id=along(to),
+            device_id_type=MESH,
+        )
+        made.start()
+        return made
+
+    for d in range(1, chips):
+        to = lax.rem(chip + d, chips) * 2 + core
+        started.append(state_copy(st.at[(chip + d) // chips], me, to, d))
+    started.append(state_copy(st.at[core], me, chip * 2 + 1 - core, 0))
 
     cb = nt(b, c)
     after = []
@@ -270,19 +339,28 @@
     grad_c = nn(b_t, dgx_sum.astype(BF16))
     inside = nn(strict, after, HIGH) - nt(strict, before, HIGH)
 
+    for d in range(1, chips):
+        slot = lax.rem(chip + d, chips) * 2 + core
+        landed(strecv, s_send, s_recv, slot, peer).wait_recv()
+        started.append(
+            state_copy(strecv.at[slot], slot, chip * 2 + 1 - core, chips - 1 + d)
+        )
+    layer.second()
+    layer.relay()
+    for d in range(1, tm):
+        landed(dec, d_send, d_recv, lax.rem(me + d, tm), peer).wait_recv()
+    for d in range(chips):
+        slot = lax.rem(chip + d, chips) * 2 + 1 - core
+        landed(strecv, s_send, s_recv, slot, peer).wait_recv()
     hin[...] = jnp.zeros_like(hin)
     gout[...] = jnp.zeros_like(gout)
 
     def forward(q, _):
-        landed(dec, d_send, d_recv, q, peer).wait_recv()
-        landed(strecv, s_send, s_recv, q, peer).wait_recv()
         hin[...] = hin[...] * jnp.exp(dec[q][0:1, :]) + strecv[q].astype(F32)
         return 0
 
     def backward(k, _):
         q = tm - 1 - k
-        landed(dec, d_send, d_recv, q, peer).wait_recv()
-        landed(strecv, s_send, s_recv, q, peer).wait_recv()
         gout[...] = gout[...] * jnp.exp(dec[q][0:1, :]) + strecv[q].astype(F32)
         return 0
 
@@ -305,8 +383,7 @@
     through = nt(jnp.broadcast_to(through, (8, width)), spread, HIGH)
     gl_ref[...] = (
         inside + nn(upper, earlier, HIGH) + nn(strict, later, HIGH) + through[0:1, :]
-    )
-    layer.near()
+    ).T
 
     for d in range(1, heads):
         landed(grecv, g_send, g_recv, lax.rem(z + d, heads), peer).wait_recv()
@@ -323,6 +400,7 @@
             turned.append(piece.astype(F32).T.astype(BF16))
     started += exchange(lambda d, to: gall.at[to], grow, a_send, a_recv, tm, me, along)
     grow[me] = gall[me]
+    layer.near()
     layer.far()
     grad_bc = jnp.concatenate(turned, axis=1)
     gi_ref[...] = nn(grad_bc, wbuf[...].reshape(tm * rows_w, wbuf.shape[2])).astype(BF16)
@@ -337,8 +415,21 @@
 
     for made in started:
         made.wait_send()
+    for made in sent:
+        for to, copy in made:
+            pl.when(to != z)(copy.wait_send)
     weights.finish()
     layer.finish()
+
+
+def store(*refs):
+    sems = refs[-1]
+    count = (len(refs) - 1) // 2
+    copies = [pltpu.make_async_copy(refs[k], refs[count + k], sems.at[k]) for k in range(count)]
+    for made in copies:
+        made.start()
+    for made in copies:
+        made.wait()
 
 
 def solution(mesh):
@@ -356,21 +447,26 @@
         copies = 14 if chips == 4 else 4 * (chips - 1) + 2
         dma = lambda *shape: pltpu.SemaphoreType.DMA(shape)
         vmem = pl.BlockSpec(memory_space=pltpu.VMEM)
+        hbm = pl.BlockSpec(memory_space=pltpu.HBM)
+        shapes = (
+            jax.ShapeDtypeStruct((span, width), F32),
+            jax.ShapeDtypeStruct((heads_here, span), F32),
+            jax.ShapeDtypeStruct((span, depth), BF16),
+            jax.ShapeDtypeStruct((rows_w, depth), F32),
+        )
 
         def body(*refs):
             kernel(tm, heads, members, *refs)
 
-        return pl.pallas_call(
+        results = pl.pallas_call(
             body,
-            out_shape=(
-                jax.ShapeDtypeStruct((span, width), F32),
-                jax.ShapeDtypeStruct((span, heads_here), F32),
-                jax.ShapeDtypeStruct((span, depth), BF16),
-                jax.ShapeDtypeStruct((rows_w, depth), F32),
-            ),
-            in_specs=[vmem] * 5,
+            out_shape=tuple(pltpu.VMEM(k.shape, k.dtype) for k in shapes),
+            in_specs=[hbm] * 5,
             out_specs=(vmem,) * 4,
             scratch_shapes=[
+                pltpu.VMEM((span, width), F32),
+                pltpu.VMEM((span, width), F32),
+                pltpu.VMEM((heads_here, span), F32),
                 pltpu.VMEM((tm, rows_w, depth), BF16),
                 pltpu.VMEM((tm, span, depth), BF16),
                 pltpu.VMEM((tm, 8, width), F32),
@@ -389,15 +485,24 @@
                 dma(copies), dma(tm, 2),
                 dma(copies), dma(tm, 2),
                 dma(tm), dma(tm),
-                dma(heads), dma(heads),
+                dma(chips, members), dma(heads, 2),
                 dma(tm), dma(tm),
                 dma(heads), dma(heads),
                 dma(tm), dma(tm),
+                dma(5),
             ],
             compiler_params=pltpu.CompilerParams(
-                collective_id=0, has_side_effects=True, vmem_limit_bytes=48 * 1024 * 1024
+                collective_id=0, has_side_effects=True, vmem_limit_bytes=56 * 1024 * 1024
             ),
-        )(layer_input, proj_weight, ssd_input, log_decay, out_grad)
+        )(layer_input, proj_weight, ssd_input, log_decay.T, out_grad)
+        grad_x, grad_log, grad_input, grad_weight = pl.pallas_call(
+            store,
+            out_shape=shapes,
+            in_specs=[vmem] * 4,
+            out_specs=(hbm,) * 4,
+            scratch_shapes=[dma(4)],
+        )(*results)
+        return grad_x, grad_log.T, grad_input, grad_weight
 
     return jax.shard_map(
         on_device,

time: 62.6 us -> 53.8 us (0.86); the launches traced: 61.7 us -> 53.6 us
  local copies, waits for them, and re-layouts: 7.62 us -> 2.85 us
  Pallas kernels: 53.4 us -> 50.1 us
    unnamed x12 -> x8, local copies, waits for them, and re-layouts: 6.96 us -> 2.85 us
    pallas_call x1 -> x2, Pallas kernels: 53.4 us -> 50.1 us  [the longest x1 47.8 us: on_device(): pl.pallas_call(body, out_shape=tuple((pltpu.VMEM(k.shape, k.dtype) for k...]
    pallas_call x1 -> x0, local copies, waits for them, and re-layouts: 0.66 us -> none  [on_device(): pl.pallas_call(body, out_shape=(jax.ShapeDtypeStruct((span, width), F32),...]
where the time goes in v2:
time: 53.8 us; the launch traced here: 53.6 us
  Pallas kernels  50.1 us (93%)
  local copies, waits for them, and re-layouts  2.85 us (5%)
  between operations  0.65 us (1%)
    pallas_call x1, Pallas kernels, on_device(): pl.pallas_call(body, out_shape=tuple((pltpu.VMEM(k.shape, k.dtype) for k...  47.8 us
    unnamed x8, local copies, waits for them, and re-layouts  2.85 us
    pallas_call x1, Pallas kernels, on_device(): pl.pallas_call(store, out_shape=shapes, in_specs=[vmem] * 4, out_specs=(h...  2.37 us

profile of v2, /device:TPU:1, one launch (start us, length us, event | category | flops | bytes accessed | tf_op | source)
XLA Modules:
  0.0 53.6 jit_solution(11347120975441411068)
XLA Ops:
  0.6 47.8 %shard_map.84 = (f32[128,512]{1,0:T(8,128)S(1)}, f32[8,128]{1,0:T(8,128)S(1)}, bf16[128,2048]{1,0:T(8,128)(2,1)S(1)}, f32[64,2048]{1,0:T(8,128)S(1)}) custom-call(bf16[128,2048]{1,0:T(8,128)(2,1)} %refs_0_.1, bf16[64,2048]{1,0:T(8,128)(2,1)} %refs_1_.1, f32[128,512]{1,0:T(8,128)} %refs_2_.1, f32[8,128]{1,0:T(8,128)} %bitcast.2, f32[128,512]{1,0:T(8,128)} %refs_4_.1), custom_call_target="tpu_custom_call" | custom-call | tf_op jit(solution)/shard_map/pallas_call | solution.py:461
  48.4 0.0 copy-start
  48.4 0.8 %copy-done = bf16[128,2048]{1,0:T(8,128)(2,1)} copy-done((bf16[128,2048]{1,0:T(8,128)(2,1)}, bf16[128,2048]{1,0:T(8,128)(2,1)S(1)}, u32[]{:S(2)}) %copy-start) | copy-done | bytes 524312
  49.2 0.0 copy-start.1
  49.2 0.8 %copy-done.1 = f32[64,2048]{1,0:T(8,128)} copy-done((f32[64,2048]{1,0:T(8,128)}, f32[64,2048]{1,0:T(8,128)S(1)}, u32[]{:S(2)}) %copy-start.1) | copy-done | bytes 524312
  50.0 0.0 copy-start.2
  50.0 0.7 %copy-done.2 = f32[128,512]{1,0:T(8,128)} copy-done((f32[128,512]{1,0:T(8,128)}, f32[128,512]{1,0:T(8,128)S(1)}, u32[]{:S(2)}) %copy-start.2) | copy-done | bytes 262168
  50.7 0.0 copy-start.3
  50.7 0.6 %copy-done.3 = f32[8,128]{1,0:T(8,128)} copy-done((f32[8,128]{1,0:T(8,128)}, f32[8,128]{1,0:T(8,128)S(1)}, u32[]{:S(2)}) %copy-start.3) | copy-done | bytes 4120
  51.3 2.4 %shard_map.85 = (f32[128,512]{1,0:T(8,128)}, f32[8,128]{1,0:T(8,128)}, bf16[128,2048]{1,0:T(8,128)(2,1)}, f32[64,2048]{1,0:T(8,128)}) custom-call(f32[128,512]{1,0:T(8,128)} %copy-done.2, f32[8,128]{1,0:T(8,128)} %copy-done.3, bf16[128,2048]{1,0:T(8,128)(2,1)} %copy-done, f32[64,2048]{1,0:T(8,128)} %copy-done.1), custom_call_target="tpu_custom_call" | custom-call | tf_op jit(solution)/shard_map/pallas_call | solution.py:498
Async XLA Ops:
  48.4 0.8 %copy-start = (bf16[128,2048]{1,0:T(8,128)(2,1)}, bf16[128,2048]{1,0:T(8,128)(2,1)S(1)}, u32[]{:S(2)}) copy-start(bf16[128,2048]{1,0:T(8,128)(2,1)S(1)} %get-tuple-element.14.refs_2_) | copy-start | bytes 1572868
  49.2 0.8 %copy-start.1 = (f32[64,2048]{1,0:T(8,128)}, f32[64,2048]{1,0:T(8,128)S(1)}, u32[]{:S(2)}) copy-start(f32[64,2048]{1,0:T(8,128)S(1)} %get-tuple-element.15.refs_3_) | copy-start | bytes 1572868
  50.0 0.7 %copy-start.2 = (f32[128,512]{1,0:T(8,128)}, f32[128,512]{1,0:T(8,128)S(1)}, u32[]{:S(2)}) copy-start(f32[128,512]{1,0:T(8,128)S(1)} %get-tuple-element.12.refs_0_) | copy-start | bytes 786436
  50.7 0.6 %copy-start.3 = (f32[8,128]{1,0:T(8,128)}, f32[8,128]{1,0:T(8,128)S(1)}, u32[]{:S(2)}) copy-start(f32[8,128]{1,0:T(8,128)S(1)} %get-tuple-element.13.refs_1_) | copy-start | bytes 12292

commit v3 on v2

--- a/solution.py
+++ b/solution.py
@@ -397,12 +397,18 @@
             first = (2 * g + part) * N // rows_w
             for k in range(N // rows_w):
                 gall[first + k] = piece[k * rows_w : (k + 1) * rows_w]
-            turned.append(piece.astype(F32).T.astype(BF16))
-    started += exchange(lambda d, to: gall.at[to], grow, a_send, a_recv, tm, me, along)
+            turned.append(piece)
+    last = exchange(lambda d, to: gall.at[to], grow, a_send, a_recv, tm, me, along)
     grow[me] = gall[me]
+    grad_bc = jnp.concatenate([k.astype(F32).T.astype(BF16) for k in turned], axis=1)
+    for made in started:
+        made.wait_send()
+    for made in sent:
+        for to, copy in made:
+            pl.when(to != z)(copy.wait_send)
+    weights.finish()
     layer.near()
     layer.far()
-    grad_bc = jnp.concatenate(turned, axis=1)
     gi_ref[...] = nn(grad_bc, wbuf[...].reshape(tm * rows_w, wbuf.shape[2])).astype(BF16)
 
     layer.other(layer.chip)
@@ -413,12 +419,8 @@
     rows = jnp.concatenate([grow[k] for k in range(tm)], axis=1)
     gw_ref[...] = nn(rows, libuf[...].reshape(tm * span, libuf.shape[2]))
 
-    for made in started:
+    for made in last:
         made.wait_send()
-    for made in sent:
-        for to, copy in made:
-            pl.when(to != z)(copy.wait_send)
-    weights.finish()
     layer.finish()
 
 
@@ -501,6 +503,7 @@
             in_specs=[vmem] * 4,
             out_specs=(hbm,) * 4,
             scratch_shapes=[dma(4)],
+            compiler_params=pltpu.CompilerParams(vmem_limit_bytes=1024 * 1024),
         )(*results)
         return grad_x, grad_log.T, grad_input, grad_weight
 

time: 53.8 us -> 49.6 us (0.922)
  local copies, waits for them, and re-layouts: 2.85 us -> 0 us
  Pallas kernels: 50.1 us -> 48.8 us
    unnamed x8 -> x0, local copies, waits for them, and re-layouts: 2.85 us -> none
    pallas_call x1, Pallas kernels: 2.37 us -> 1.09 us  [on_device(): pl.pallas_call(store, out_shape=shapes, in_specs=[vmem] * 4, out_specs=(h...]
where the time goes in v3:
time: 49.6 us; the launch traced here: 49.4 us
  Pallas kernels  48.8 us (98%)
  between operations  0.64 us (1%)
    pallas_call x1, Pallas kernels, on_device(): pl.pallas_call(body, out_shape=tuple((pltpu.VMEM(k.shape, k.dtype) for k...  47.7 us
    pallas_call x1, Pallas kernels, on_device(): pl.pallas_call(store, out_shape=shapes, in_specs=[vmem] * 4, out_specs=(h...  1.09 us

profile of v3, /device:TPU:1, one launch (start us, length us, event | category | flops | bytes accessed | tf_op | source)
XLA Modules:
  0.0 49.4 jit_solution(7076879599305161559)
XLA Ops:
  0.6 47.7 %shard_map.84 = (f32[128,512]{1,0:T(8,128)S(1)}, f32[8,128]{1,0:T(8,128)S(1)}, bf16[128,2048]{1,0:T(8,128)(2,1)S(1)}, f32[64,2048]{1,0:T(8,128)S(1)}) custom-call(bf16[128,2048]{1,0:T(8,128)(2,1)} %refs_0_.1, bf16[64,2048]{1,0:T(8,128)(2,1)} %refs_1_.1, f32[128,512]{1,0:T(8,128)} %refs_2_.1, f32[8,128]{1,0:T(8,128)} %bitcast.2, f32[128,512]{1,0:T(8,128)} %refs_4_.1), custom_call_target="tpu_custom_call" | custom-call | tf_op jit(solution)/shard_map/pallas_call | solution.py:463
  48.3 1.1 %shard_map.85 = (f32[128,512]{1,0:T(8,128)}, f32[8,128]{1,0:T(8,128)}, bf16[128,2048]{1,0:T(8,128)(2,1)}, f32[64,2048]{1,0:T(8,128)}) custom-call(f32[128,512]{1,0:T(8,128)S(1)} %get-tuple-element.12.refs_0_, f32[8,128]{1,0:T(8,128)S(1)} %get-tuple-element.13.refs_1_, bf16[128,2048]{1,0:T(8,128)(2,1)S(1)} %get-tuple-element.14.refs_2_, ...), custom_call_target="tpu_custom_call" | custom-call | tf_op jit(solution)/shard_map/pallas_call | solution.py:500

commit v4 on v3

--- a/solution.py
+++ b/solution.py
@@ -60,29 +60,17 @@
     def arrive(self, slot, half):
         self.copy(slot, half, self.chip, 1 - self.core, 0).wait_recv()
 
-    def start(self):
-        self.first()
-        self.second()
-
-    def first(self):
+    def out(self):
         me, core = self.me, self.core
         if self.chips == 4:
             self.push(me, 0, self.xn, core)
             self.push(me, 1, self.yn, core)
-        else:
-            for d in range(1, self.chips):
-                self.push(me, 0, lax.rem(self.chip + d, self.chips), core)
-        for half in range(2):
-            self.push(me, half, self.chip, 1 - core)
-
-    def second(self):
-        me, core = self.me, self.core
-        if self.chips == 4:
             self.push(me, 1, self.xn, core)
             self.push(me, 0, self.yn, core)
         else:
             for d in range(1, self.chips):
-                self.push(me, 1, lax.rem(self.chip + d, self.chips), core)
+                for half in range(2):
+                    self.push(me, half, lax.rem(self.chip + d, self.chips), core)
 
     def relay(self):
         core = self.core
@@ -92,28 +80,31 @@
             self.push(xs, 0, self.yn, core)
             self.arrive(ys, 1)
             self.push(ys, 1, self.xn, core)
-            self.push(xs, 0, self.chip, 1 - core)
-            self.push(ys, 1, self.chip, 1 - core)
 
     def near(self):
-        core = self.core
+        if self.chips != 4:
+            return []
+        xs, ys = self.xn * 2 + self.core, self.yn * 2 + self.core
+        self.arrive(xs, 1)
+        self.arrive(ys, 0)
+        return [xs, ys]
+
+    def far(self):
         if self.chips == 4:
-            xs, ys = self.xn * 2 + core, self.yn * 2 + core
-            self.arrive(xs, 1)
-            self.push(xs, 1, self.chip, 1 - core)
-            self.arrive(ys, 0)
-            self.push(ys, 0, self.chip, 1 - core)
-
-    def far(self):
-        core = self.core
-        if self.chips == 4:
-            slots = [self.dg * 2 + core]
+            slots = [self.dg * 2 + self.core]
         else:
-            slots = [lax.rem(self.chip + d, self.chips) * 2 + core for d in range(1, self.chips)]
+            slots = [
+                lax.rem(self.chip + d, self.chips) * 2 + self.core for d in range(1, self.chips)
+            ]
         for slot in slots:
             for half in range(2):
                 self.arrive(slot, half)
-                self.push(slot, half, self.chip, 1 - core)
+        return slots
+
+    def share(self, slots):
+        for slot in slots:
+            for half in range(2):
+                self.push(slot, half, self.chip, 1 - self.core)
 
     def other(self, chip):
         for half in range(2):
@@ -159,7 +150,7 @@
     li_hbm, w_hbm, x_hbm, log_hbm, dy_hbm,
     gx_ref, gl_ref, gi_ref, gw_ref,
     x_ref, dy_ref, log_ref,
-    wbuf, libuf, dec, pbuf, bcr, st, strecv, hin, gout, decay, dgx, gbuf, grecv, gall, grow,
+    wbuf, libuf, dec, pbuf, bcr, st, strecv, hin, gout, decay, dgx, grecv, gall, grow,
     w_send, w_recv, li_send, li_recv, d_send, d_recv, p_send, p_recv, s_send, s_recv,
     g_send, g_recv, a_send, a_recv, in_sem,
 ):
@@ -184,6 +175,7 @@
     ]
     for made in loads:
         made.start()
+    chip, core = me // 2, lax.rem(me, 2)
     barrier = pltpu.get_barrier_semaphore()
     for d in range(1, tm):
         pl.semaphore_signal(
@@ -192,6 +184,12 @@
     for d in range(1, heads):
         pl.semaphore_signal(
             barrier, inc=1, device_id=across_z(lax.rem(z + d, heads)), device_id_type=MESH
+        )
+        pl.semaphore_signal(
+            barrier,
+            inc=1,
+            device_id=(chip * 2 + 1 - core, lax.rem(z + d, heads)),
+            device_id_type=MESH,
         )
 
     weights = Gather(wbuf, w_send, w_recv, tm, me, z)
@@ -213,8 +211,10 @@
     total = wide[span - 1 : span, :]
     dec[me] = jnp.broadcast_to(total, (8, width))
     loads[1].wait()
-    pl.semaphore_wait(barrier, tm - 1 + heads - 1)
-    weights.start()
+    pl.semaphore_wait(barrier, tm - 1 + 2 * (heads - 1))
+    weights.out()
+    loads[4].wait()
+    layer.share([me])
     started += exchange(lambda d, to: dec.at[me], dec, d_send, d_recv, tm, me, along)
     loads[2].wait()
     loads[3].wait()
@@ -227,85 +227,90 @@
     x_half = x.astype(BF16)
     dy_half = dy.astype(BF16)
 
-    weights.relay()
-
     dgx_sum = jnp.zeros((span, span), F32)
-    for h in range(heads_here):
+
+    def pairs_of(h, so_far):
         cut = slice(h * size, (h + 1) * size)
         gaps = sums_t[h : h + 1, :] - sums[:, h : h + 1]
         step = jnp.where(row <= col, jnp.exp(jnp.minimum(gaps, 0.0)), 0.0)
         pairs = step * nt(x_half[:, cut], dy_half[:, cut])
         decay[h] = step
         dgx[h] = pairs
-        dgx_sum = dgx_sum + pairs
-
-    loads[4].wait()
+        return so_far + pairs
+
+    for h in range(heads_here // 2):
+        dgx_sum = pairs_of(h, dgx_sum)
+    weights.relay()
+
     sent = []
 
-    def project(chip):
+    def project(slot):
         number = len(sent)
-        block = wbuf[pl.ds(2 * chip, 2)].reshape(2 * rows_w, wbuf.shape[2])
-        pbuf[chip] = nt(libuf[me], block).astype(BF16)
-        part = lax.rem(chip, 2)
+        k = slot // 2
+        steps = libuf[pl.ds(2 * chip, 2)].reshape(2 * span, libuf.shape[2])
+        rows = nt(wbuf[slot], steps).astype(BF16)
+        pbuf[k, 0] = rows[:, :span]
+        pbuf[k, 1] = rows[:, span:]
+        part = lax.rem(k, 2)
         made = []
         for m in range(members):
-            to = chip // 2 * members + m
-            made.append((to, pltpu.make_async_remote_copy(
-                src_ref=pbuf.at[chip],
-                dst_ref=bcr.at[z, part],
-                send_sem=p_send.at[number, m],
-                recv_sem=p_recv.at[z, part],
-                device_id=across_z(to),
-                device_id_type=MESH,
-            )))
+            to = k // 2 * members + m
+            for away in range(2):
+                side = core if away == 0 else 1 - core
+                made.append((to != z if away == 0 else None, pltpu.make_async_remote_copy(
+                    src_ref=pbuf.at[k, side],
+                    dst_ref=bcr.at[z, part, core],
+                    send_sem=p_send.at[number, 2 * m + away],
+                    recv_sem=p_recv.at[z, 2 * part + core],
+                    device_id=(chip * 2 + side, to),
+                    device_id_type=MESH,
+                )))
         sent.append(made)
-        for to, copy in made:
-            pl.when(to != z)(copy.start)
-
-    weights.near()
-    weights.other(weights.chip)
-    project(weights.chip)
-    if chips == 4:
-        weights.other(weights.xn)
-        project(weights.xn)
-        weights.other(weights.yn)
-        project(weights.yn)
-        weights.far()
-        layer.first()
-        weights.other(weights.dg)
-        project(weights.dg)
-    else:
-        weights.far()
-        layer.first()
-        for d in range(1, chips):
-            chip = lax.rem(weights.chip + d, chips)
-            weights.other(chip)
-            project(chip)
+        for goes, copy in made:
+            if goes is None:
+                copy.start()
+            else:
+                pl.when(goes)(copy.start)
+
+    layer.other(chip)
+    project(me)
+    for h in range(heads_here // 2, heads_here):
+        dgx_sum = pairs_of(h, dgx_sum)
+    held = weights.near()
+    for slot in held:
+        project(slot)
+    layer.out()
+    rest = weights.far()
+    for slot in rest:
+        project(slot)
     group = z // members
-    bcr[z] = pbuf[pl.ds(2 * group, 2)]
+    for part in range(2):
+        bcr[z, part, core] = pbuf[2 * group + part, core]
+
+    def bc_landed(source, place):
+        pltpu.make_async_remote_copy(
+            src_ref=bcr.at[source, place // 2, lax.rem(place, 2)],
+            dst_ref=bcr.at[source, place // 2, lax.rem(place, 2)],
+            send_sem=p_send.at[0, 0],
+            recv_sem=p_recv.at[source, place],
+            device_id=peer,
+            device_id_type=MESH,
+        ).wait_recv()
+
+    for part in range(2):
+        bc_landed(z, 2 * part + 1 - core)
     for d in range(1, heads):
-        other = lax.rem(z + d, heads)
-        for part in range(2):
-            pltpu.make_async_remote_copy(
-                src_ref=bcr.at[other, part],
-                dst_ref=bcr.at[other, part],
-                send_sem=p_send.at[0, 0],
-                recv_sem=p_recv.at[other, part],
-                device_id=peer,
-                device_id_type=MESH,
-            ).wait_recv()
+        for k in range(4):
+            bc_landed(lax.rem(z + d, heads), k)
     bc = bcr[0].astype(F32)
     for k in range(1, heads):
         bc = bc + bcr[k].astype(F32)
-    b_t = bc[0].T.astype(BF16)
-    c_t = bc[1].T.astype(BF16)
-    b = bc[0].astype(BF16)
-    c = bc[1].astype(BF16)
+    bc = bc.reshape(2, N, span)
+    b_t = bc[0].astype(BF16)
+    c_t = bc[1].astype(BF16)
 
     st[0] = nn(b_t, x_end).astype(BF16)
     st[1] = nn(c_t, dy_start).astype(BF16)
-    chip, core = me // 2, lax.rem(me, 2)
-
     def state_copy(src, slot, to, number):
         made = pltpu.make_async_remote_copy(
             src_ref=src,
@@ -322,6 +327,10 @@
         to = lax.rem(chip + d, chips) * 2 + core
         started.append(state_copy(st.at[(chip + d) // chips], me, to, d))
     started.append(state_copy(st.at[core], me, chip * 2 + 1 - core, 0))
+
+    weights.share([me] + held + rest)
+    b = bc[0].T.astype(BF16)
+    c = bc[1].T.astype(BF16)
 
     cb = nt(b, c)
     after = []
@@ -345,7 +354,6 @@
         started.append(
             state_copy(strecv.at[slot], slot, chip * 2 + 1 - core, chips - 1 + d)
         )
-    layer.second()
     layer.relay()
     for d in range(1, tm):
         landed(dec, d_send, d_recv, lax.rem(me + d, tm), peer).wait_recv()
@@ -364,16 +372,31 @@
         gout[...] = gout[...] * jnp.exp(dec[q][0:1, :]) + strecv[q].astype(F32)
         return 0
 
+    def send_grad(part, value):
+        grecv[z, part] = value.astype(BF16)
+        copies = []
+        for d in range(1, heads):
+            copies.append(pltpu.make_async_remote_copy(
+                src_ref=grecv.at[z, part],
+                dst_ref=grecv.at[z, part],
+                send_sem=g_send.at[d, part],
+                recv_sem=g_recv.at[z, part],
+                device_id=across_z(lax.rem(z + d, heads)),
+                device_id_type=MESH,
+            ))
+        for made in copies:
+            made.start()
+        return copies
+
+    lax.fori_loop(0, tm - 1 - me, backward, 0)
+    grad = gout[...]
+    grad_half = grad.astype(BF16)
+    started += send_grad(0, grad_b + nt(grad_half, x_end))
     lax.fori_loop(0, me, forward, 0)
-    lax.fori_loop(0, tm - 1 - me, backward, 0)
     state = hin[...]
-    grad = gout[...]
     state_half = state.astype(BF16)
-    grad_half = grad.astype(BF16)
-    gbuf[0] = (grad_b + nt(grad_half, x_end)).astype(BF16)
-    gbuf[1] = (grad_c + nt(state_half, dy_start)).astype(BF16)
-    grecv[z] = gbuf[...]
-    started += exchange(lambda d, to: gbuf, grecv, g_send, g_recv, heads, z, across_z)
+    started += send_grad(1, grad_c + nt(state_half, dy_start))
+    layer.share(layer.near())
 
     from_end = to_end * nn(b, grad_half)
     gx_ref[...] += from_end
@@ -386,7 +409,16 @@
     ).T
 
     for d in range(1, heads):
-        landed(grecv, g_send, g_recv, lax.rem(z + d, heads), peer).wait_recv()
+        other = lax.rem(z + d, heads)
+        for part in range(2):
+            pltpu.make_async_remote_copy(
+                src_ref=grecv.at[other, part],
+                dst_ref=grecv.at[other, part],
+                send_sem=g_send.at[0, 0],
+                recv_sem=g_recv.at[other, part],
+                device_id=peer,
+                device_id_type=MESH,
+            ).wait_recv()
     turned = []
     for g in range(heads // members):
         for part in range(2):
@@ -400,18 +432,21 @@
             turned.append(piece)
     last = exchange(lambda d, to: gall.at[to], grow, a_send, a_recv, tm, me, along)
     grow[me] = gall[me]
+    layer.share(layer.far())
     grad_bc = jnp.concatenate([k.astype(F32).T.astype(BF16) for k in turned], axis=1)
     for made in started:
         made.wait_send()
     for made in sent:
-        for to, copy in made:
-            pl.when(to != z)(copy.wait_send)
+        for goes, copy in made:
+            if goes is None:
+                copy.wait_send()
+            else:
+                pl.when(goes)(copy.wait_send)
+    for k in range(chips):
+        weights.other(k)
     weights.finish()
-    layer.near()
-    layer.far()
     gi_ref[...] = nn(grad_bc, wbuf[...].reshape(tm * rows_w, wbuf.shape[2])).astype(BF16)
 
-    layer.other(layer.chip)
     for d in range(1, chips):
         layer.other(lax.rem(layer.chip + d, chips))
     for d in range(1, tm):
@@ -472,24 +507,23 @@
                 pltpu.VMEM((tm, rows_w, depth), BF16),
                 pltpu.VMEM((tm, span, depth), BF16),
                 pltpu.VMEM((tm, 8, width), F32),
-                pltpu.VMEM((chips, span, N), BF16),
-                pltpu.VMEM((heads, 2, span, N), BF16),
+                pltpu.VMEM((chips, 2, rows_w, span), BF16),
+                pltpu.VMEM((heads, 2, 2, rows_w, span), BF16),
                 pltpu.VMEM((2, N, width), BF16),
                 pltpu.VMEM((tm, N, width), BF16),
                 pltpu.VMEM((N, width), F32),
                 pltpu.VMEM((N, width), F32),
                 pltpu.VMEM((heads_here, span, span), F32),
                 pltpu.VMEM((heads_here, span, span), F32),
-                pltpu.VMEM((2, N, span), BF16),
                 pltpu.VMEM((heads, 2, N, span), BF16),
                 pltpu.VMEM((tm, rows_w, span), BF16),
                 pltpu.VMEM((tm, rows_w, span), BF16),
                 dma(copies), dma(tm, 2),
                 dma(copies), dma(tm, 2),
                 dma(tm), dma(tm),
-                dma(chips, members), dma(heads, 2),
+                dma(chips, 2 * members), dma(heads, 4),
                 dma(tm), dma(tm),
-                dma(heads), dma(heads),
+                dma(heads, 2), dma(heads, 2),
                 dma(tm), dma(tm),
                 dma(5),
             ],

time: 49.6 us -> 50.7 us (1.022)
  Pallas kernels: 48.8 us -> 49.5 us
    pallas_call x1, Pallas kernels: 47.7 us -> 48.4 us  [on_device(): pl.pallas_call(body, out_shape=tuple((pltpu.VMEM(k.shape, k.dtype) for k...]
where the time goes in v4:
time: 50.7 us; the launch traced here: 50.2 us
  Pallas kernels  49.5 us (98%)
  between operations  0.64 us (1%)
    pallas_call x1, Pallas kernels, on_device(): pl.pallas_call(body, out_shape=tuple((pltpu.VMEM(k.shape, k.dtype) for k...  48.4 us
    pallas_call x1, Pallas kernels, on_device(): pl.pallas_call(store, out_shape=shapes, in_specs=[vmem] * 4, out_specs=(h...  1.09 us

profile of v4, /device:TPU:1, one launch (start us, length us, event | category | flops | bytes accessed | tf_op | source)
XLA Modules:
  0.0 50.2 jit_solution(2872235421206293308)
XLA Ops:
  0.6 48.4 %shard_map.84 = (f32[128,512]{1,0:T(8,128)S(1)}, f32[8,128]{1,0:T(8,128)S(1)}, bf16[128,2048]{1,0:T(8,128)(2,1)S(1)}, f32[64,2048]{1,0:T(8,128)S(1)}) custom-call(bf16[128,2048]{1,0:T(8,128)(2,1)} %refs_0_.1, bf16[64,2048]{1,0:T(8,128)(2,1)} %refs_1_.1, f32[128,512]{1,0:T(8,128)} %refs_2_.1, f32[8,128]{1,0:T(8,128)} %bitcast.2, f32[128,512]{1,0:T(8,128)} %refs_4_.1), custom_call_target="tpu_custom_call" | custom-call | tf_op jit(solution)/shard_map/pallas_call | solution.py:498
  49.1 1.1 %shard_map.85 = (f32[128,512]{1,0:T(8,128)}, f32[8,128]{1,0:T(8,128)}, bf16[128,2048]{1,0:T(8,128)(2,1)}, f32[64,2048]{1,0:T(8,128)}) custom-call(f32[128,512]{1,0:T(8,128)S(1)} %get-tuple-element.12.refs_0_, f32[8,128]{1,0:T(8,128)S(1)} %get-tuple-element.13.refs_1_, bf16[128,2048]{1,0:T(8,128)(2,1)S(1)} %get-tuple-element.14.refs_2_, ...), custom_call_target="tpu_custom_call" | custom-call | tf_op jit(solution)/shard_map/pallas_call | solution.py:534

commit v5 on v4

--- a/solution.py
+++ b/solution.py
@@ -61,16 +61,26 @@
         self.copy(slot, half, self.chip, 1 - self.core, 0).wait_recv()
 
     def out(self):
+        self.first()
+        self.second()
+
+    def first(self):
         me, core = self.me, self.core
         if self.chips == 4:
             self.push(me, 0, self.xn, core)
             self.push(me, 1, self.yn, core)
+        else:
+            for d in range(1, self.chips):
+                self.push(me, 0, lax.rem(self.chip + d, self.chips), core)
+
+    def second(self):
+        me, core = self.me, self.core
+        if self.chips == 4:
             self.push(me, 1, self.xn, core)
             self.push(me, 0, self.yn, core)
         else:
             for d in range(1, self.chips):
-                for half in range(2):
-                    self.push(me, half, lax.rem(self.chip + d, self.chips), core)
+                self.push(me, 1, lax.rem(self.chip + d, self.chips), core)
 
     def relay(self):
         core = self.core
@@ -279,10 +289,10 @@
     held = weights.near()
     for slot in held:
         project(slot)
-    layer.out()
     rest = weights.far()
     for slot in rest:
         project(slot)
+    layer.first()
     group = z // members
     for part in range(2):
         bcr[z, part, core] = pbuf[2 * group + part, core]
@@ -354,6 +364,7 @@
         started.append(
             state_copy(strecv.at[slot], slot, chip * 2 + 1 - core, chips - 1 + d)
         )
+    layer.second()
     layer.relay()
     for d in range(1, tm):
         landed(dec, d_send, d_recv, lax.rem(me + d, tm), peer).wait_recv()
@@ -396,7 +407,6 @@
     state = hin[...]
     state_half = state.astype(BF16)
     started += send_grad(1, grad_c + nt(state_half, dy_start))
-    layer.share(layer.near())
 
     from_end = to_end * nn(b, grad_half)
     gx_ref[...] += from_end
@@ -432,6 +442,7 @@
             turned.append(piece)
     last = exchange(lambda d, to: gall.at[to], grow, a_send, a_recv, tm, me, along)
     grow[me] = gall[me]
+    layer.share(layer.near())
     layer.share(layer.far())
     grad_bc = jnp.concatenate([k.astype(F32).T.astype(BF16) for k in turned], axis=1)
     for made in started:

time: 50.7 us -> 50.4 us (level)
  no operation moved by 1% of the time
where the time goes in v5:
time: 50.4 us; the launch traced here: 50.2 us
  Pallas kernels  49.6 us (98%)
  between operations  0.64 us (1%)
    pallas_call x1, Pallas kernels, on_device(): pl.pallas_call(body, out_shape=tuple((pltpu.VMEM(k.shape, k.dtype) for k...  48.5 us
    pallas_call x1, Pallas kernels, on_device(): pl.pallas_call(store, out_shape=shapes, in_specs=[vmem] * 4, out_specs=(h...  1.09 us

profile of v5, /device:TPU:1, one launch (start us, length us, event | category | flops | bytes accessed | tf_op | source)
XLA Modules:
  0.0 50.2 jit_solution(14265167017324207282)
XLA Ops:
  0.6 48.5 %shard_map.84 = (f32[128,512]{1,0:T(8,128)S(1)}, f32[8,128]{1,0:T(8,128)S(1)}, bf16[128,2048]{1,0:T(8,128)(2,1)S(1)}, f32[64,2048]{1,0:T(8,128)S(1)}) custom-call(bf16[128,2048]{1,0:T(8,128)(2,1)} %refs_0_.1, bf16[64,2048]{1,0:T(8,128)(2,1)} %refs_1_.1, f32[128,512]{1,0:T(8,128)} %refs_2_.1, f32[8,128]{1,0:T(8,128)} %bitcast.2, f32[128,512]{1,0:T(8,128)} %refs_4_.1), custom_call_target="tpu_custom_call" | custom-call | tf_op jit(solution)/shard_map/pallas_call | solution.py:509
  49.1 1.1 %shard_map.85 = (f32[128,512]{1,0:T(8,128)}, f32[8,128]{1,0:T(8,128)}, bf16[128,2048]{1,0:T(8,128)(2,1)}, f32[64,2048]{1,0:T(8,128)}) custom-call(f32[128,512]{1,0:T(8,128)S(1)} %get-tuple-element.12.refs_0_, f32[8,128]{1,0:T(8,128)S(1)} %get-tuple-element.13.refs_1_, bf16[128,2048]{1,0:T(8,128)(2,1)S(1)} %get-tuple-element.14.refs_2_, ...), custom_call_target="tpu_custom_call" | custom-call | tf_op jit(solution)/shard_map/pallas_call | solution.py:545

commit v6 on v5

--- a/solution.py
+++ b/solution.py
@@ -160,7 +160,7 @@
     li_hbm, w_hbm, x_hbm, log_hbm, dy_hbm,
     gx_ref, gl_ref, gi_ref, gw_ref,
     x_ref, dy_ref, log_ref,
-    wbuf, libuf, dec, pbuf, bcr, st, strecv, hin, gout, decay, dgx, grecv, gall, grow,
+    wbuf, libuf, dec, pbuf, bcr, st, strecv, hin, gout, decay, dgx, lit, grecv, gall, grow,
     w_send, w_recv, li_send, li_recv, d_send, d_recv, p_send, p_recv, s_send, s_recv,
     g_send, g_recv, a_send, a_recv, in_sem,
 ):
@@ -232,8 +232,13 @@
     to_end = jnp.exp(total - wide)
     x = x_ref[...]
     dy = dy_ref[...]
-    x_end = (to_end * x).astype(BF16)
-    dy_start = (from_start * dy).astype(BF16)
+    x_end = to_end * x
+    dy_start = from_start * dy
+    x_end_t = x_end.T.astype(BF16)
+    dy_start_t = dy_start.T.astype(BF16)
+    x_end = x_end.astype(BF16)
+    dy_start = dy_start.astype(BF16)
+    lit[:, :span] = libuf[me].T
     x_half = x.astype(BF16)
     dy_half = dy.astype(BF16)
 
@@ -248,8 +253,6 @@
         dgx[h] = pairs
         return so_far + pairs
 
-    for h in range(heads_here // 2):
-        dgx_sum = pairs_of(h, dgx_sum)
     weights.relay()
 
     sent = []
@@ -257,8 +260,7 @@
     def project(slot):
         number = len(sent)
         k = slot // 2
-        steps = libuf[pl.ds(2 * chip, 2)].reshape(2 * span, libuf.shape[2])
-        rows = nt(wbuf[slot], steps).astype(BF16)
+        rows = nn(wbuf[slot], lit[...]).astype(BF16)
         pbuf[k, 0] = rows[:, :span]
         pbuf[k, 1] = rows[:, span:]
         part = lax.rem(k, 2)
@@ -268,7 +270,7 @@
             for away in range(2):
                 side = core if away == 0 else 1 - core
                 made.append((to != z if away == 0 else None, pltpu.make_async_remote_copy(
-                    src_ref=pbuf.at[k, side],
+                    src_ref=pbuf.at[k, away],
                     dst_ref=bcr.at[z, part, core],
                     send_sem=p_send.at[number, 2 * m + away],
                     recv_sem=p_recv.at[z, 2 * part + core],
@@ -283,8 +285,9 @@
                 pl.when(goes)(copy.start)
 
     layer.other(chip)
+    lit[:, span:] = libuf[chip * 2 + 1 - core].T
     project(me)
-    for h in range(heads_here // 2, heads_here):
+    for h in range(heads_here):
         dgx_sum = pairs_of(h, dgx_sum)
     held = weights.near()
     for slot in held:
@@ -295,7 +298,7 @@
     layer.first()
     group = z // members
     for part in range(2):
-        bcr[z, part, core] = pbuf[2 * group + part, core]
+        bcr[z, part, core] = pbuf[2 * group + part, 0]
 
     def bc_landed(source, place):
         pltpu.make_async_remote_copy(
@@ -342,7 +345,7 @@
     b = bc[0].T.astype(BF16)
     c = bc[1].T.astype(BF16)
 
-    cb = nt(b, c)
+    cb = nn(b, c_t)
     after = []
     before = []
     for h in range(heads_here):
@@ -402,11 +405,11 @@
     lax.fori_loop(0, tm - 1 - me, backward, 0)
     grad = gout[...]
     grad_half = grad.astype(BF16)
-    started += send_grad(0, grad_b + nt(grad_half, x_end))
+    started += send_grad(0, grad_b + nn(grad_half, x_end_t))
     lax.fori_loop(0, me, forward, 0)
     state = hin[...]
     state_half = state.astype(BF16)
-    started += send_grad(1, grad_c + nt(state_half, dy_start))
+    started += send_grad(1, grad_c + nn(state_half, dy_start_t))
 
     from_end = to_end * nn(b, grad_half)
     gx_ref[...] += from_end
@@ -526,6 +529,7 @@
                 pltpu.VMEM((N, width), F32),
                 pltpu.VMEM((heads_here, span, span), F32),
                 pltpu.VMEM((heads_here, span, span), F32),
+                pltpu.VMEM((depth, 2 * span), BF16),
                 pltpu.VMEM((heads, 2, N, span), BF16),
                 pltpu.VMEM((tm, rows_w, span), BF16),
                 pltpu.VMEM((tm, rows_w, span), BF16),

time: 50.4 us -> 50.2 us (level)
  no operation moved by 1% of the time
where the time goes in v6:
time: 50.2 us; the launch traced here: 50 us
  Pallas kernels  49.4 us (98%)
  between operations  0.64 us (1%)
    pallas_call x1, Pallas kernels, on_device(): pl.pallas_call(body, out_shape=tuple((pltpu.VMEM(k.shape, k.dtype) for k...  48.3 us
    pallas_call x1, Pallas kernels, on_device(): pl.pallas_call(store, out_shape=shapes, in_specs=[vmem] * 4, out_specs=(h...  1.09 us

profile of v6, /device:TPU:1, one launch (start us, length us, event | category | flops | bytes accessed | tf_op | source)
XLA Modules:
  0.0 50.0 jit_solution(162496902418035811)
XLA Ops:
  0.6 48.3 %shard_map.84 = (f32[128,512]{1,0:T(8,128)S(1)}, f32[8,128]{1,0:T(8,128)S(1)}, bf16[128,2048]{1,0:T(8,128)(2,1)S(1)}, f32[64,2048]{1,0:T(8,128)S(1)}) custom-call(bf16[128,2048]{1,0:T(8,128)(2,1)} %refs_0_.1, bf16[64,2048]{1,0:T(8,128)(2,1)} %refs_1_.1, f32[128,512]{1,0:T(8,128)} %refs_2_.1, f32[8,128]{1,0:T(8,128)} %bitcast.2, f32[128,512]{1,0:T(8,128)} %refs_4_.1), custom_call_target="tpu_custom_call" | custom-call | tf_op jit(solution)/shard_map/pallas_call | solution.py:512
  48.9 1.1 %shard_map.85 = (f32[128,512]{1,0:T(8,128)}, f32[8,128]{1,0:T(8,128)}, bf16[128,2048]{1,0:T(8,128)(2,1)}, f32[64,2048]{1,0:T(8,128)}) custom-call(f32[128,512]{1,0:T(8,128)S(1)} %get-tuple-element.12.refs_0_, f32[8,128]{1,0:T(8,128)S(1)} %get-tuple-element.13.refs_1_, bf16[128,2048]{1,0:T(8,128)(2,1)S(1)} %get-tuple-element.14.refs_2_, ...), custom_call_target="tpu_custom_call" | custom-call | tf_op jit(solution)/shard_map/pallas_call | solution.py:549

commit v7 on v6

--- a/solution.py
+++ b/solution.py
@@ -160,7 +160,7 @@
     li_hbm, w_hbm, x_hbm, log_hbm, dy_hbm,
     gx_ref, gl_ref, gi_ref, gw_ref,
     x_ref, dy_ref, log_ref,
-    wbuf, libuf, dec, pbuf, bcr, st, strecv, hin, gout, decay, dgx, lit, grecv, gall, grow,
+    wbuf, libuf, dec, pbuf, bcr, st, sibst, agg, strecv, hin, gout, decay, dgx, lit, grecv, gall, grow,
     w_send, w_recv, li_send, li_recv, d_send, d_recv, p_send, p_recv, s_send, s_recv,
     g_send, g_recv, a_send, a_recv, in_sem,
 ):
@@ -324,23 +324,45 @@
 
     st[0] = nn(b_t, x_end).astype(BF16)
     st[1] = nn(c_t, dy_start).astype(BF16)
-    def state_copy(src, slot, to, number):
-        made = pltpu.make_async_remote_copy(
+    half = width // 2
+    sibling = chip * 2 + 1 - core
+
+    def state_copy(src, dst, to, number, place):
+        return pltpu.make_async_remote_copy(
             src_ref=src,
-            dst_ref=strecv.at[slot],
+            dst_ref=dst,
             send_sem=s_send.at[number],
-            recv_sem=s_recv.at[slot],
+            recv_sem=s_recv.at[place],
             device_id=along(to),
             device_id_type=MESH,
         )
-        made.start()
-        return made
-
+
+    swap = state_copy(st, sibst, sibling, 0, 2 * chip)
+    swap.start()
+    started.append(swap)
+    for d in range(1, tm):
+        landed(dec, d_send, d_recv, lax.rem(me + d, tm), peer).wait_recv()
+    mine = pl.ds(pl.multiple_of(core * half, half), half)
+    own_decay = jnp.exp(dec[me, 0:1, mine])
+    sib_decay = jnp.exp(dec[sibling, 0:1, mine])
+    one = jnp.ones_like(own_decay)
+    first = core == 0
+    swap.wait_recv()
+    agg[0] = (
+        jnp.where(first, sib_decay, one) * st[0, :, mine].astype(F32)
+        + jnp.where(first, one, own_decay) * sibst[0, :, mine].astype(F32)
+    ).astype(BF16)
+    agg[1] = (
+        jnp.where(first, one, sib_decay) * st[1, :, mine].astype(F32)
+        + jnp.where(first, own_decay, one) * sibst[1, :, mine].astype(F32)
+    ).astype(BF16)
     for d in range(1, chips):
         to = lax.rem(chip + d, chips) * 2 + core
-        started.append(state_copy(st.at[(chip + d) // chips], me, to, d))
-    started.append(state_copy(st.at[core], me, chip * 2 + 1 - core, 0))
-
+        made = state_copy(
+            agg.at[(chip + d) // chips], strecv.at[me], to, d, me
+        )
+        made.start()
+        started.append(made)
     weights.share([me] + held + rest)
     b = bc[0].T.astype(BF16)
     c = bc[1].T.astype(BF16)
@@ -364,27 +386,33 @@
     for d in range(1, chips):
         slot = lax.rem(chip + d, chips) * 2 + core
         landed(strecv, s_send, s_recv, slot, peer).wait_recv()
-        started.append(
-            state_copy(strecv.at[slot], slot, chip * 2 + 1 - core, chips - 1 + d)
-        )
+        made = state_copy(strecv.at[slot], strecv.at[slot], sibling, chips - 1 + d, slot)
+        made.start()
+        started.append(made)
     layer.second()
     layer.relay()
-    for d in range(1, tm):
-        landed(dec, d_send, d_recv, lax.rem(me + d, tm), peer).wait_recv()
-    for d in range(chips):
+    for d in range(1, chips):
         slot = lax.rem(chip + d, chips) * 2 + 1 - core
         landed(strecv, s_send, s_recv, slot, peer).wait_recv()
     hin[...] = jnp.zeros_like(hin)
     gout[...] = jnp.zeros_like(gout)
 
+    def fold(ref, q):
+        decays = jnp.exp(dec[2 * q][0:1, :] + dec[2 * q + 1][0:1, :])
+        for k in range(2):
+            cut = slice(k * half, (k + 1) * half)
+            ref[:, cut] = ref[:, cut] * decays[:, cut] + strecv[2 * q + k].astype(F32)
+
     def forward(q, _):
-        hin[...] = hin[...] * jnp.exp(dec[q][0:1, :]) + strecv[q].astype(F32)
+        fold(hin, q)
         return 0
 
     def backward(k, _):
-        q = tm - 1 - k
-        gout[...] = gout[...] * jnp.exp(dec[q][0:1, :]) + strecv[q].astype(F32)
+        fold(gout, chips - 1 - k)
         return 0
+
+    def fold_sibling(ref, part):
+        ref[...] = ref[...] * jnp.exp(dec[sibling][0:1, :]) + sibst[part].astype(F32)
 
     def send_grad(part, value):
         grecv[z, part] = value.astype(BF16)
@@ -402,11 +430,13 @@
             made.start()
         return copies
 
-    lax.fori_loop(0, tm - 1 - me, backward, 0)
+    lax.fori_loop(0, chips - 1 - chip, backward, 0)
+    pl.when(core == 0)(lambda: fold_sibling(gout, 1))
     grad = gout[...]
     grad_half = grad.astype(BF16)
     started += send_grad(0, grad_b + nn(grad_half, x_end_t))
-    lax.fori_loop(0, me, forward, 0)
+    lax.fori_loop(0, chip, forward, 0)
+    pl.when(core == 1)(lambda: fold_sibling(hin, 0))
     state = hin[...]
     state_half = state.astype(BF16)
     started += send_grad(1, grad_c + nn(state_half, dy_start_t))
@@ -524,7 +554,9 @@
                 pltpu.VMEM((chips, 2, rows_w, span), BF16),
                 pltpu.VMEM((heads, 2, 2, rows_w, span), BF16),
                 pltpu.VMEM((2, N, width), BF16),
-                pltpu.VMEM((tm, N, width), BF16),
+                pltpu.VMEM((2, N, width), BF16),
+                pltpu.VMEM((2, N, width // 2), BF16),
+                pltpu.VMEM((tm, N, width // 2), BF16),
                 pltpu.VMEM((N, width), F32),
                 pltpu.VMEM((N, width), F32),
                 pltpu.VMEM((heads_here, span, span), F32),

time: 50.2 us -> 48.2 us (0.960)
  Pallas kernels: 49.4 us -> 47.4 us
    pallas_call x1, Pallas kernels: 48.3 us -> 46.3 us  [on_device(): pl.pallas_call(body, out_shape=tuple((pltpu.VMEM(k.shape, k.dtype) for k...]
where the time goes in v7:
time: 48.2 us; the launch traced here: 48.1 us
  Pallas kernels  47.4 us (98%)
  between operations  0.64 us (1%)
    pallas_call x1, Pallas kernels, on_device(): pl.pallas_call(body, out_shape=tuple((pltpu.VMEM(k.shape, k.dtype) for k...  46.3 us
    pallas_call x1, Pallas kernels, on_device(): pl.pallas_call(store, out_shape=shapes, in_specs=[vmem] * 4, out_specs=(h...  1.09 us

profile of v7, /device:TPU:1, one launch (start us, length us, event | category | flops | bytes accessed | tf_op | source)
XLA Modules:
  0.0 48.1 jit_solution(5752760922804123798)
XLA Ops:
  0.6 46.3 %shard_map.84 = (f32[128,512]{1,0:T(8,128)S(1)}, f32[8,128]{1,0:T(8,128)S(1)}, bf16[128,2048]{1,0:T(8,128)(2,1)S(1)}, f32[64,2048]{1,0:T(8,128)S(1)}) custom-call(bf16[128,2048]{1,0:T(8,128)(2,1)} %refs_0_.1, bf16[64,2048]{1,0:T(8,128)(2,1)} %refs_1_.1, f32[128,512]{1,0:T(8,128)} %refs_2_.1, f32[8,128]{1,0:T(8,128)} %bitcast.2, f32[128,512]{1,0:T(8,128)} %refs_4_.1), custom_call_target="tpu_custom_call" | custom-call | tf_op jit(solution)/shard_map/pallas_call | solution.py:542
  47.0 1.1 %shard_map.85 = (f32[128,512]{1,0:T(8,128)}, f32[8,128]{1,0:T(8,128)}, bf16[128,2048]{1,0:T(8,128)(2,1)}, f32[64,2048]{1,0:T(8,128)}) custom-call(f32[128,512]{1,0:T(8,128)S(1)} %get-tuple-element.12.refs_0_, f32[8,128]{1,0:T(8,128)S(1)} %get-tuple-element.13.refs_1_, bf16[128,2048]{1,0:T(8,128)(2,1)S(1)} %get-tuple-element.14.refs_2_, ...), custom_call_target="tpu_custom_call" | custom-call | tf_op jit(solution)/shard_map/pallas_call | solution.py:581

commit v8 on v7

--- a/solution.py
+++ b/solution.py
@@ -38,11 +38,14 @@
             self.yn = lax.rem(chip + 2, 4)
             self.dg = 3 - chip
 
-    def piece(self, slot, half):
-        return self.buf.at[slot, pl.ds(half * self.half_rows, self.half_rows)]
-
-    def copy(self, slot, half, chip, core, number):
-        part = self.piece(slot, half)
+    def piece(self, slot, half, quarter):
+        if quarter is None:
+            return self.buf.at[slot, pl.ds(half * self.half_rows, self.half_rows)]
+        rows = self.half_rows // 2
+        return self.buf.at[slot, pl.ds((2 * half + quarter) * rows, rows)]
+
+    def copy(self, slot, half, chip, core, number, quarter=None):
+        part = self.piece(slot, half, quarter)
         return pltpu.make_async_remote_copy(
             src_ref=part,
             dst_ref=part,
@@ -52,8 +55,8 @@
             device_id_type=MESH,
         )
 
-    def push(self, slot, half, chip, core):
-        made = self.copy(slot, half, chip, core, len(self.pending))
+    def push(self, slot, half, chip, core, quarter=None):
+        made = self.copy(slot, half, chip, core, len(self.pending), quarter)
         made.start()
         self.pending.append(made)
 
@@ -73,14 +76,14 @@
             for d in range(1, self.chips):
                 self.push(me, 0, lax.rem(self.chip + d, self.chips), core)
 
-    def second(self):
+    def second(self, quarter=None):
         me, core = self.me, self.core
         if self.chips == 4:
-            self.push(me, 1, self.xn, core)
-            self.push(me, 0, self.yn, core)
+            self.push(me, 1, self.xn, core, quarter)
+            self.push(me, 0, self.yn, core, quarter)
         else:
             for d in range(1, self.chips):
-                self.push(me, 1, lax.rem(self.chip + d, self.chips), core)
+                self.push(me, 1, lax.rem(self.chip + d, self.chips), core, quarter)
 
     def relay(self):
         core = self.core
@@ -339,6 +342,7 @@
 
     swap = state_copy(st, sibst, sibling, 0, 2 * chip)
     swap.start()
+    layer.second(0)
     started.append(swap)
     for d in range(1, tm):
         landed(dec, d_send, d_recv, lax.rem(me + d, tm), peer).wait_recv()
@@ -389,8 +393,8 @@
         made = state_copy(strecv.at[slot], strecv.at[slot], sibling, chips - 1 + d, slot)
         made.start()
         started.append(made)
-    layer.second()
     layer.relay()
+    layer.second(1)
     for d in range(1, chips):
         slot = lax.rem(chip + d, chips) * 2 + 1 - core
         landed(strecv, s_send, s_recv, slot, peer).wait_recv()
@@ -566,7 +570,7 @@
                 pltpu.VMEM((tm, rows_w, span), BF16),
                 pltpu.VMEM((tm, rows_w, span), BF16),
                 dma(copies), dma(tm, 2),
-                dma(copies), dma(tm, 2),
+                dma(copies + chips), dma(tm, 2),
                 dma(tm), dma(tm),
                 dma(chips, 2 * members), dma(heads, 4),
                 dma(tm), dma(tm),

time: 48.2 us -> 47.9 us (level)
  no operation moved by 1% of the time
where the time goes in v8:
time: 47.9 us; the launch traced here: 47.7 us
  Pallas kernels  47.1 us (98%)
  between operations  0.64 us (1%)
    pallas_call x1, Pallas kernels, on_device(): pl.pallas_call(body, out_shape=tuple((pltpu.VMEM(k.shape, k.dtype) for k...  46 us
    pallas_call x1, Pallas kernels, on_device(): pl.pallas_call(store, out_shape=shapes, in_specs=[vmem] * 4, out_specs=(h...  1.09 us

profile of v8, /device:TPU:1, one launch (start us, length us, event | category | flops | bytes accessed | tf_op | source)
XLA Modules:
  0.0 47.7 jit_solution(14873908587768287346)
XLA Ops:
  0.6 46.0 %shard_map.84 = (f32[128,512]{1,0:T(8,128)S(1)}, f32[8,128]{1,0:T(8,128)S(1)}, bf16[128,2048]{1,0:T(8,128)(2,1)S(1)}, f32[64,2048]{1,0:T(8,128)S(1)}) custom-call(bf16[128,2048]{1,0:T(8,128)(2,1)} %refs_0_.1, bf16[64,2048]{1,0:T(8,128)(2,1)} %refs_1_.1, f32[128,512]{1,0:T(8,128)} %refs_2_.1, f32[8,128]{1,0:T(8,128)} %bitcast.2, f32[128,512]{1,0:T(8,128)} %refs_4_.1), custom_call_target="tpu_custom_call" | custom-call | tf_op jit(solution)/shard_map/pallas_call | solution.py:546
  46.6 1.1 %shard_map.85 = (f32[128,512]{1,0:T(8,128)}, f32[8,128]{1,0:T(8,128)}, bf16[128,2048]{1,0:T(8,128)(2,1)}, f32[64,2048]{1,0:T(8,128)}) custom-call(f32[128,512]{1,0:T(8,128)S(1)} %get-tuple-element.12.refs_0_, f32[8,128]{1,0:T(8,128)S(1)} %get-tuple-element.13.refs_1_, bf16[128,2048]{1,0:T(8,128)(2,1)S(1)} %get-tuple-element.14.refs_2_, ...), custom_call_target="tpu_custom_call" | custom-call | tf_op jit(solution)/shard_map/pallas_call | solution.py:585

commit v9 on v8

--- a/solution.py
+++ b/solution.py
@@ -367,7 +367,6 @@
         )
         made.start()
         started.append(made)
-    weights.share([me] + held + rest)
     b = bc[0].T.astype(BF16)
     c = bc[1].T.astype(BF16)
 
@@ -444,6 +443,7 @@
     state = hin[...]
     state_half = state.astype(BF16)
     started += send_grad(1, grad_c + nn(state_half, dy_start_t))
+    weights.share([me] + held + rest)
 
     from_end = to_end * nn(b, grad_half)
     gx_ref[...] += from_end

time: 47.9 us -> 47.9 us (level)
  no operation moved by 1% of the time
where the time goes in v9:
time: 47.9 us; the launch traced here: 47.7 us
  Pallas kernels  47.1 us (98%)
  between operations  0.64 us (1%)
    pallas_call x1, Pallas kernels, on_device(): pl.pallas_call(body, out_shape=tuple((pltpu.VMEM(k.shape, k.dtype) for k...  46 us
    pallas_call x1, Pallas kernels, on_device(): pl.pallas_call(store, out_shape=shapes, in_specs=[vmem] * 4, out_specs=(h...  1.09 us

profile of v9, /device:TPU:1, one launch (start us, length us, event | category | flops | bytes accessed | tf_op | source)
XLA Modules:
  0.0 47.7 jit_solution(11988164899991624302)
XLA Ops:
  0.6 46.0 %shard_map.84 = (f32[128,512]{1,0:T(8,128)S(1)}, f32[8,128]{1,0:T(8,128)S(1)}, bf16[128,2048]{1,0:T(8,128)(2,1)S(1)}, f32[64,2048]{1,0:T(8,128)S(1)}) custom-call(bf16[128,2048]{1,0:T(8,128)(2,1)} %refs_0_.1, bf16[64,2048]{1,0:T(8,128)(2,1)} %refs_1_.1, f32[128,512]{1,0:T(8,128)} %refs_2_.1, f32[8,128]{1,0:T(8,128)} %bitcast.2, f32[128,512]{1,0:T(8,128)} %refs_4_.1), custom_call_target="tpu_custom_call" | custom-call | tf_op jit(solution)/shard_map/pallas_call | solution.py:546
  46.6 1.1 %shard_map.85 = (f32[128,512]{1,0:T(8,128)}, f32[8,128]{1,0:T(8,128)}, bf16[128,2048]{1,0:T(8,128)(2,1)}, f32[64,2048]{1,0:T(8,128)}) custom-call(f32[128,512]{1,0:T(8,128)S(1)} %get-tuple-element.12.refs_0_, f32[8,128]{1,0:T(8,128)S(1)} %get-tuple-element.13.refs_1_, bf16[128,2048]{1,0:T(8,128)(2,1)S(1)} %get-tuple-element.14.refs_2_, ...), custom_call_target="tpu_custom_call" | custom-call | tf_op jit(solution)/shard_map/pallas_call | solution.py:585
